TPU v7x, 32 devices: a whole 2x2x4 slice. The times are simulated.
32 devices in a mesh: flow: 2 (over x), col: 4 (over y, core), row: 4 (over z).
Axes of the slice: x: 2, y: 2, z: 4, core: 2. Of those that a mesh axis runs over, the one named last changes fastest.
Arguments:
- forcing: float32 [5, 12, 48, 768], P(None, 'flow', 'col', 'row'), may hold values from -6 to 6
- previous: float32 [5, 12, 48, 768], P(None, 'flow', 'col', 'row'), may hold values from -6 to 6
- element_diagonal_shift: float32 [2, 8, 128], P('flow', 'col', 'row'), may hold values from 0.5 to 4
- eigen_bases: float32 [3, 6, 6], replicated, may hold values from -1 to 1, as said below
- eigen_values: float32 [3, 6], replicated, may hold values from 0.5 to 8
- observers: float32 [3, 256], replicated, may hold values from 8 to 30
- panel_points: float32 [3, 1024], P(None, ('flow', 'col', 'row')), may hold values from -2 to 2
- surface_history: float32 [4, 15, 1024], P(None, None, ('flow', 'col', 'row')), may hold values from -6 to 6
Outputs:
- new_state: float32 [5, 12, 48, 768], P(None, 'flow', 'col', 'row')
- spectra: float32 [2, 16, 256], P(None, None, 'row')
Inputs may be any that keep to these rules, and one draw needn't show every extreme that they name: Each eigen_bases[d] is an orthogonal matrix.
All inputs are finite; a program needn't handle non-finite values.
Results may differ from a plain program's by a relative error of at most 0.0003.
Values sent between devices are 32-bit elements; how exact they have to be, the bound alone decides.
A program may use at most 64 MiB of HBM per device.

v0:
```python
import math

import jax
import jax.numpy as jnp
from jax import lax
from jax.sharding import PartitionSpec as P

P_SIZE = 6
SWEEPS = 2
NT = 16
NF = 16


HIGH = lax.Precision.HIGHEST
OMEGA = 0.8
TAU = 0.5
KMAX = 2.0


def with_halo(x, sides, width):
    for axis, dim in sides:
        size, length = (lax.axis_size(axis), x.shape[dim])
        up = [(i, (i + 1) % size) for i in range(size - 1)]
        down = [(j, i) for i, j in up]
        last = lax.slice_in_dim(x, length - width, length, axis=dim)
        first = lax.slice_in_dim(x, 0, width, axis=dim)
        before = lax.ppermute(last, axis, up)
        after = lax.ppermute(first, axis, down)
        x = jnp.concatenate([before, x, after], axis=dim)
    return x


def contract_small(field, matrix, which):
    extent = field.shape
    count = extent[which]
    blocked = field.reshape(extent[:which] + (count // P_SIZE, P_SIZE) + extent[which + 1 :])
    blocked = jnp.moveaxis(blocked, which + 1, -1)
    result = jnp.einsum("...p,qp->...q", blocked, matrix, precision=HIGH)
    result = jnp.moveaxis(result, -1, which + 1)
    return result.reshape(extent)


def contract_last(field, wide_matrix):
    extent = field.shape
    group = wide_matrix.shape[0]
    blocked = field.reshape(extent[0], extent[1], extent[2], extent[3] // group, group)
    result = jnp.einsum("cxybg,hg->cxybh", blocked, wide_matrix, precision=HIGH)
    return result.reshape(extent)


def face_masks(count):
    index = jnp.arange(count) % P_SIZE
    return ((index == P_SIZE - 1).astype(jnp.float32), (index == 0).astype(jnp.float32))


def far_terms(observers, points, source_re, source_im):
    offsets = observers[:, :, None] - points[:, None, :]
    radius = jnp.sqrt(jnp.sum(offsets * offsets, axis=0))
    unit_dir = offsets / radius[None]
    freqs = source_re.shape[1]
    wavenum = (KMAX * (jnp.arange(freqs, dtype=jnp.float32) + 0.5) / freqs)[:, None, None]
    along_re = (
        unit_dir[0][None] * source_re[1][:, None, :]
        + unit_dir[1][None] * source_re[2][:, None, :]
        + unit_dir[2][None] * source_re[3][:, None, :]
    )
    along_im = (
        unit_dir[0][None] * source_im[1][:, None, :]
        + unit_dir[1][None] * source_im[2][:, None, :]
        + unit_dir[2][None] * source_im[3][:, None, :]
    )
    inverse_matrix = 1.0 / radius[None]
    term_re = -wavenum * (source_im[0][:, None, :] + along_im) + along_re * inverse_matrix
    term_im = wavenum * (source_re[0][:, None, :] + along_re) + along_im * inverse_matrix
    phases = wavenum * radius[None]
    amplitude = inverse_matrix / (4.0 * math.pi)
    green_re = amplitude * jnp.cos(phases)
    green_im = -amplitude * jnp.sin(phases)
    total_re = jnp.sum(green_re * term_re - green_im * term_im, axis=2)
    total_im = jnp.sum(green_re * term_im + green_im * term_re, axis=2)
    return jnp.stack([total_re, total_im])


def transform(samples):
    times = jnp.arange(NT, dtype=jnp.float32)
    omegas = math.pi * (jnp.arange(NF, dtype=jnp.float32) + 0.5) / NF
    cos_table = jnp.cos(omegas[:, None] * times[None, :])
    sin_table = jnp.sin(omegas[:, None] * times[None, :])
    source_re = jnp.einsum("fn,cnp->cfp", cos_table, samples, precision=HIGH)
    source_im = -jnp.einsum("fn,cnp->cfp", sin_table, samples, precision=HIGH)
    return (source_re, source_im)


def on_device(
    forcing,
    previous,
    element_diagonal_shift,
    eigen_bases,
    eigen_values,
    observers,
    panel_points,
    surface_history,
):
    extent = forcing.shape
    stiffness = [
        jnp.dot(
            eigen_bases[axis_num] * eigen_values[axis_num][None, :],
            eigen_bases[axis_num].T,
            precision=HIGH,
        )
        for axis_num in range(3)
    ]
    group = P_SIZE * math.gcd(extent[3] // P_SIZE, 64)
    identity = jnp.eye(group // P_SIZE, dtype=jnp.float32)
    wide_stiff = jnp.kron(identity, stiffness[2])
    wide_forward = jnp.kron(identity, eigen_bases[2].T)
    wide_back = jnp.kron(identity, eigen_bases[2])
    shift_nodes = jnp.repeat(
        jnp.repeat(jnp.repeat(element_diagonal_shift, P_SIZE, 0), P_SIZE, 1), P_SIZE, 2
    )
    denominator = (
        shift_nodes
        + jnp.tile(eigen_values[0], extent[1] // P_SIZE)[:, None, None]
        + jnp.tile(eigen_values[1], extent[2] // P_SIZE)[None, :, None]
        + jnp.tile(eigen_values[2], extent[3] // P_SIZE)[None, None, :]
    )
    high_x, low_x = face_masks(extent[1])
    high_y, low_y = face_masks(extent[2])
    high_z, low_z = face_masks(extent[3])
    state = previous
    for sweep in range(SWEEPS):
        apply_result = shift_nodes[None] * state + contract_small(state, stiffness[0], 1)
        apply_result = apply_result + contract_small(state, stiffness[1], 2)
        padded = with_halo(state, (("flow", 1), ("col", 2), ("row", 3)), 1)
        next_x = padded[:, 2:, 1:-1, 1:-1]
        prev_x = padded[:, :-2, 1:-1, 1:-1]
        next_y = padded[:, 1:-1, 2:, 1:-1]
        prev_y = padded[:, 1:-1, :-2, 1:-1]
        next_z = padded[:, 1:-1, 1:-1, 2:]
        prev_z = padded[:, 1:-1, 1:-1, :-2]
        result = high_x[None, :, None, None] * next_x + low_x[None, :, None, None] * prev_x
        result = result + high_y[None, None, :, None] * next_y + low_y[None, None, :, None] * prev_y
        residual = (
            forcing
            - (apply_result + contract_last(state, wide_stiff))
            + TAU
            * (result + high_z[None, None, None, :] * next_z + low_z[None, None, None, :] * prev_z)
        )
        block_result = contract_small(residual, eigen_bases[0].T, 1)
        block_result = contract_small(block_result, eigen_bases[1].T, 2)
        block_result = contract_last(block_result, wide_forward) / denominator[None]
        block_result = contract_small(block_result, eigen_bases[0], 1)
        block_result = contract_small(block_result, eigen_bases[1], 2)
        state = state + OMEGA * contract_last(block_result, wide_back)
    own_panels = panel_points.shape[1]
    newest = state[:4, 0, 0, :own_panels]
    surface_samples = jnp.concatenate([surface_history, newest[:, None, :]], axis=1)
    rows = lax.axis_size("row")
    count = observers.shape[1] // rows
    points, samples = (
        lax.all_gather(panel_points, "row", axis=1, tiled=True),
        lax.all_gather(surface_samples, "row", axis=2, tiled=True),
    )
    source_re, source_im = transform(samples)
    own_obs = lax.dynamic_slice_in_dim(observers, lax.axis_index("row") * count, count, 1)
    partial_sums = far_terms(own_obs, points, source_re, source_im)
    spectra = lax.psum(partial_sums, ("flow", "col"))
    return (state, spectra)


def solution(mesh):
    return jax.shard_map(
        on_device,
        mesh=mesh,
        in_specs=(
            P(None, "flow", "col", "row"),
            P(None, "flow", "col", "row"),
            P("flow", "col", "row"),
            P(),
            P(),
            P(),
            P(None, ("flow", "col", "row")),
            P(None, None, ("flow", "col", "row")),
        ),
        out_specs=(P(None, "flow", "col", "row"), P(None, None, "row")),
        check_vma=False,
    )
```

profile of v0, /device:TPU:0, one launch (start us, length us, event | category | flops | bytes accessed | tf_op | source)
XLA Modules:
  0.0 143.8 jit_solution(3606890502460777156)
XLA Ops:
  0.6 0.9 fusion.168
  1.7 1.3 collective-permute-start
  3.0 4.8 %collective-permute-start.1 = (f32[5,1,12,192]{3,1,2,0:T(1,128)S(1)}, f32[5,1,12,192]{3,1,2,0:T(1,128)S(1)}, u32[]{:S(2)}, u32[]{:S(2)}) collective-permute-start(f32[5,1,12,192]{3,1,2,0:T(1,128)S(1)} %copy.139), channel_id=1, source_target_pairs={{0,16},{1,17},{2,18},{3,19},{4,20},{5,21},{6,22},{7,23},{8,24},{9,... | collective-permute-start | bytes 138248 | tf_op jit(solution)/shard_map/ppermute | solution.py:27
  7.9 1.3 copy.153
  9.2 0.7 slice_bitcast_fusion.12
  10.0 0.8 slice_bitcast_fusion.15
  10.8 0.9 fusion.131
  11.7 4.9 %broadcast_multiply_fusion = (f32[32,6,32,6]{3,2,1,0:T(8,128)}, f32[32,6,32,6]{3,2,1,0:T(8,128)}, f32[32,6,32,6]{3,2,1,0:T(8,128)}) fusion(f32[6,6]{1,0:T(8,128)S(1)} %get-tuple-element.42, f32[32,32]{1,0:T(8,128)S(1)} %fusion.118, f32[6,6]{1,0:T(8,128)S(1)} %copy.146, f32[6,6]{1,0:T(8,128)S(1)} %fusion.131), kind=kLoop, calls=%fused_computation | loop fusion | flops 110592 | bytes 446896 | tf_op jit(solution)/shard_map/jit(kron)/mul | solution.py:117
  16.6 3.9 %reshape.301 = f32[192,192,1,1]{1,0,2,3:T(8,128)S(1)} reshape(f32[32,6,32,6]{3,2,1,0:T(8,128)} %get-tuple-element.41) | data formatting | bytes 294912 | tf_op jit(solution)/shard_map/jit(kron)/mul | solution.py:115
  20.6 0.7 convolution_bitcast_fusion.6
  22.9 13.2 %all-gather = f32[4,32,3]{1,2,0:T(4,128)S(1)} all-gather(f32[1,32,3]{1,2,0:T(4,128)S(1)} %bitcast.282), channel_id=1, replica_groups=mesh['flow'=2,'col'=4,'row'=4] {'row'}, dimensions={0}, use_global_device_ids=true | all-gather | bytes 1920 | tf_op jit(solution)/shard_map/all_gather | solution.py:161
  36.4 0.7 broadcast_multiply_fusion.3
  37.2 0.6 slice_bitcast_fusion.2
  37.8 0.7 add_add_fusion
  38.5 1.1 fusion.3
  39.7 1.3 collective-permute-start.2
  41.0 3.0 %collective-permute-start.3 = (f32[5,8,1,192]{3,1,2,0:T(8,128)S(1)}, f32[5,8,1,192]{3,1,2,0:T(8,128)S(1)}, u32[]{:S(2)}, u32[]{:S(2)}) collective-permute-start(f32[5,8,1,192]{3,1,2,0:T(8,128)S(1)} %get-tuple-element.14), channel_id=1, source_target_pairs={{0,4},{4,8},{8,12},{1,5},{5,9},{9,13},{2,6},{6,10},{10,14},{3,7},{... | collective-permute-start | bytes 92168 | tf_op jit(solution)/shard_map/ppermute | solution.py:27
  44.1 0.8 collective-permute-done.3
  45.3 4.2 %collective-permute-start.5 = (f32[5,8,14,1]{3,1,2,0:T(8,128)S(1)}, f32[5,8,14,1]{3,1,2,0:T(8,128)}, u32[]{:S(2)}, u32[]{:S(2)}) collective-permute-start(f32[5,8,14,1]{3,1,2,0:T(8,128)S(1)} %get-tuple-element.19), channel_id=1, source_target_pairs={{0,1},{1,2},{2,3},{4,5},{5,6},{6,7},{8,9},{9,10},{10,11},{12,13},{... | collective-permute-start | bytes 6728 | tf_op jit(solution)/shard_map/ppermute | solution.py:27
  49.5 1.5 %collective-permute-start.4 = (f32[5,8,14,1]{3,1,2,0:T(8,128)S(1)}, f32[5,8,14,1]{3,1,2,0:T(8,128)}, u32[]{:S(2)}, u32[]{:S(2)}) collective-permute-start(f32[5,8,14,1]{3,1,2,0:T(8,128)S(1)} %get-tuple-element.18), channel_id=1, source_target_pairs={{1,0},{2,1},{3,2},{5,4},{6,5},{7,6},{9,8},{10,9},{11,10},{13,12},{... | collective-permute-start | bytes 6728 | tf_op jit(solution)/shard_map/ppermute | solution.py:28
  51.0 3.9 %reshape.304 = f32[192,192,1,1]{1,0,2,3:T(8,128)S(1)} reshape(f32[32,6,32,6]{3,2,1,0:T(8,128)} %get-tuple-element.40) | data formatting | bytes 294912 | tf_op jit(solution)/shard_map/jit(kron)/mul | solution.py:116
  54.8 3.9 %reshape.307 = f32[192,192,1,1]{1,0,2,3:T(8,128)S(1)} reshape(f32[32,6,32,6]{3,2,1,0:T(8,128)} %get-tuple-element.39) | data formatting | bytes 294912 | tf_op jit(solution)/shard_map/jit(kron)/mul | solution.py:117
  58.8 2.2 %collective-permute-done.4 = f32[5,8,14,1]{3,1,2,0:T(8,128)} collective-permute-done((f32[5,8,14,1]{3,1,2,0:T(8,128)S(1)}, f32[5,8,14,1]{3,1,2,0:T(8,128)}, u32[]{:S(2)}, u32[]{:S(2)}) %collective-permute-start.4) | collective-permute-done | bytes 2272 | tf_op jit(solution)/shard_map/ppermute | solution.py:28
  61.0 2.7 %fusion.55 = f32[5,12,192,6]{2,3,1,0:T(8,128)S(1)} fusion(f32[5,6,12,192]{3,1,2,0:T(8,128)S(1)} %fusion.3, f32[5,8,14,1]{3,1,2,0:T(8,128)} %collective-permute-done.5, f32[5,8,1,192]{3,1,2,0:T(8,128)S(1)} %collective-permute-done.2, f32[5,8,1,192]{3,1,2,0:T(8,128)S(1)} %collective-permute-done.3, f32[5,1,12,192]{3,1,2,0:T(1,128)S(1)} %collective-permute-done, ...), kind=kOutput, calls=%fused_computation.96 | convolution fusion | flops 7119360 | bytes 1476992 | tf_op jit(solution)/shard_map/...p,qp->...q/dot_general | solution.py:38
  63.8 0.6 convolution_bitcast_fusion.5
  65.3 0.8 fusion.90
  66.1 0.6 convolution_bitcast_fusion.4
  66.9 0.8 fusion.10
  67.9 1.3 collective-permute-start.6
  69.2 4.5 %collective-permute-start.7 = (f32[5,1,12,192]{3,1,2,0:T(1,128)S(1)}, f32[5,1,12,192]{3,1,2,0:T(1,128)S(1)}, u32[]{:S(2)}, u32[]{:S(2)}) collective-permute-start(f32[5,1,12,192]{3,1,2,0:T(1,128)S(1)} %get-tuple-element.20), channel_id=1, source_target_pairs={{0,16},{1,17},{2,18},{3,19},{4,20},{5,21},{6,22},{7,23},{8,24},{9,... | collective-permute-start | bytes 138248 | tf_op jit(solution)/shard_map/ppermute | solution.py:27
  73.7 0.6 fusion.114
  74.4 1.2 collective-permute-done.7
  75.6 1.3 collective-permute-start.8
  76.9 3.3 %collective-permute-start.9 = (f32[5,8,1,192]{3,1,2,0:T(8,128)S(1)}, f32[5,8,1,192]{3,1,2,0:T(8,128)S(1)}, u32[]{:S(2)}, u32[]{:S(2)}) collective-permute-start(f32[5,8,1,192]{3,1,2,0:T(8,128)S(1)} %get-tuple-element.12), channel_id=1, source_target_pairs={{0,4},{4,8},{8,12},{1,5},{5,9},{9,13},{2,6},{6,10},{10,14},{3,7},{... | collective-permute-start | bytes 92168 | tf_op jit(solution)/shard_map/ppermute | solution.py:27
  81.4 2.4 %collective-permute-start.11 = (f32[5,8,14,1]{3,1,2,0:T(8,128)S(1)}, f32[5,8,14,1]{3,1,2,0:T(8,128)S(1)}, u32[]{:S(2)}, u32[]{:S(2)}) collective-permute-start(f32[5,8,14,1]{3,1,2,0:T(8,128)S(1)} %get-tuple-element.17), channel_id=1, source_target_pairs={{0,1},{1,2},{2,3},{4,5},{5,6},{6,7},{8,9},{9,10},{10,11},{12,13},{... | collective-permute-start | bytes 6728 | tf_op jit(solution)/shard_map/ppermute | solution.py:27
  83.8 1.3 collective-permute-start.10
  85.1 0.8 fusion.7
  85.9 2.9 %collective-permute-done.11 = f32[5,8,14,1]{3,1,2,0:T(8,128)S(1)} collective-permute-done((f32[5,8,14,1]{3,1,2,0:T(8,128)S(1)}, f32[5,8,14,1]{3,1,2,0:T(8,128)S(1)}, u32[]{:S(2)}, u32[]{:S(2)}) %collective-permute-start.11) | collective-permute-done | bytes 2272 | tf_op jit(solution)/shard_map/ppermute | solution.py:27
  88.8 4.7 %collective-permute-done.10 = f32[5,8,14,1]{3,1,2,0:T(8,128)S(1)} collective-permute-done((f32[5,8,14,1]{3,1,2,0:T(8,128)S(1)}, f32[5,8,14,1]{3,1,2,0:T(8,128)S(1)}, u32[]{:S(2)}, u32[]{:S(2)}) %collective-permute-start.10) | collective-permute-done | bytes 2272 | tf_op jit(solution)/shard_map/ppermute | solution.py:28
  93.5 1.7 %fusion.28 = f32[5,12,192,6]{2,3,1,0:T(8,128)S(1)} fusion(f32[5,6,12,192]{3,1,2,0:T(8,128)S(1)} %fusion.7, f32[5,8,14,1]{3,1,2,0:T(8,128)S(1)} %collective-permute-done.11, f32[5,8,1,192]{3,1,2,0:T(8,128)S(1)} %collective-permute-done.8, f32[5,8,1,192]{3,1,2,0:T(8,128)S(1)} %collective-permute-done.9, f32[5,1,12,192]{3,1,2,0:T(1,128)S(1)} %collective-permute-done.6, ...), kind=kOutput, calls=%fused_computation.57 | convolution fusion | flops 7119360 | bytes 2045952 | tf_op jit(solution)/shard_map/...p,qp->...q/dot_general | solution.py:38
  95.2 0.6 convolution_bitcast_fusion.1
  96.7 0.8 fusion.84
  97.5 0.6 convolution_bitcast_fusion
  98.3 0.7 fusion.8
  99.0 0.9 copy.174
  100.2 14.4 %all_gather.7 = f32[4,16,128]{1,0,2:T(4,128)S(1)} all-gather(f32[4,16,32]{1,0,2:T(4,128)S(1)} %pad_maximum_fusion.62), channel_id=1, replica_groups=mesh['flow'=2,'col'=4,'row'=4] {'row'}, dimensions={2}, use_global_device_ids=true | all-gather | bytes 40960 | tf_op jit(solution)/shard_map/all_gather | solution.py:162
  115.4 2.7 %fusion.17 = (f32[16,64]{1,0:T(8,128)S(1)}, f32[16,64]{1,0:T(8,128)S(1)}) fusion(f32[16,128]{1,0:T(8,128)S(1)} %get-tuple-element.36, f32[64,128]{1,0:T(8,128)S(1)} %copy-done.6, f32[64,128]{1,0:T(8,128)S(1)} %copy-done.7, f32[16,128]{1,0:T(8,128)S(1)} %get-tuple-element.37, f32[16,128]{1,0:T(8,128)S(1)} %get-tuple-element.38, ...), kind=kLoop, calls=%fused_computation.41 | loop fusion | flops 3799040 | bytes 303232 | tf_op jit(solution)/shard_map/reduce_sum | solution.py:79
  118.1 25.7 %psum.7 = f32[2,16,64]{2,1,0:T(8,128)} all-reduce(f32[2,16,64]{2,1,0:T(8,128)S(1)} %pad_maximum_fusion.69), channel_id=1, replica_groups=mesh['flow'=2,'col'=4,'row'=4] {'flow','col'}, use_global_device_ids=true, to_apply=%region_3.4 | all-reduce | flops 2048 | bytes 16384 | tf_op jit(solution)/shard_map/psum | solution.py:167
  (86 shorter events, 7.0 us)
Async XLA Ops:
  0.6 35.6 %copy-start = (f32[3,256]{1,0:T(4,128)S(1)}, f32[3,256]{1,0:T(4,128)}, u32[]{:S(2)}) copy-start(f32[3,256]{1,0:T(4,128)} %param.13) | copy-start | bytes 9220
  1.7 38.0 %collective-permute-start = (f32[5,1,12,192]{3,1,2,0:T(1,128)S(1)}, f32[5,1,12,192]{3,1,2,0:T(1,128)S(1)}, u32[]{:S(2)}, u32[]{:S(2)}) collective-permute-start(f32[5,1,12,192]{3,1,2,0:T(1,128)S(1)} %copy.137), channel_id=1, source_target_pairs={{16,0},{17,1},{18,2},{19,3},{20,4},{21,5},{22,6},{23,7},{24,8},{25... | collective-permute-start | bytes 138248 | tf_op jit(solution)/shard_map/ppermute | solution.py:28
  3.0 36.6 %collective-permute-start.1 = (f32[5,1,12,192]{3,1,2,0:T(1,128)S(1)}, f32[5,1,12,192]{3,1,2,0:T(1,128)S(1)}, u32[]{:S(2)}, u32[]{:S(2)}) collective-permute-start(f32[5,1,12,192]{3,1,2,0:T(1,128)S(1)} %copy.139), channel_id=1, source_target_pairs={{0,16},{1,17},{2,18},{3,19},{4,20},{5,21},{6,22},{7,23},{8,24},{9,... | collective-permute-start | bytes 138248 | tf_op jit(solution)/shard_map/ppermute | solution.py:27
  16.6 4.0 %copy-start.1 = (f32[5,6,12,192]{3,2,1,0:T(8,128)S(1)}, f32[5,6,12,192]{3,2,1,0:T(8,128)}, u32[]{:S(2)}) copy-start(f32[5,6,12,192]{3,2,1,0:T(8,128)} %param.9) | copy-start | bytes 829444
  16.6 4.7 %copy-start.3 = (f32[3,6,6]{2,1,0:T(8,128)S(1)}, f32[3,6,6]{2,1,0:T(8,128)}, u32[]{:S(2)}) copy-start(f32[3,6,6]{2,1,0:T(8,128)} %param.11) | copy-start | bytes 1300
  16.6 5.8 %copy-start.13 = (f32[1,2,32]{2,1,0:T(2,128)S(1)}, f32[1,2,32]{2,1,0:T(2,128)}, u32[]{:S(2)}) copy-start(f32[1,2,32]{2,1,0:T(2,128)} %param.10) | copy-start | bytes 772
  16.6 6.3 %copy-start.12 = (f32[3,32]{1,0:T(4,128)S(1)}, f32[3,32]{1,0:T(4,128)}, u32[]{:S(2)}) copy-start(f32[3,32]{1,0:T(4,128)} %param.14) | copy-start | bytes 1156
  16.6 21.9 %copy-start.2 = (f32[5,6,12,192]{3,2,1,0:T(8,128)S(1)}, f32[5,6,12,192]{3,2,1,0:T(8,128)}, u32[]{:S(2)}) copy-start(f32[5,6,12,192]{3,2,1,0:T(8,128)} %param.8) | copy-start | bytes 829444
  39.7 4.4 %collective-permute-start.2 = (f32[5,8,1,192]{3,1,2,0:T(8,128)S(1)}, f32[5,8,1,192]{3,1,2,0:T(8,128)S(1)}, u32[]{:S(2)}, u32[]{:S(2)}) collective-permute-start(f32[5,8,1,192]{3,1,2,0:T(8,128)S(1)} %get-tuple-element.15), channel_id=1, source_target_pairs={{4,0},{8,4},{12,8},{5,1},{9,5},{13,9},{6,2},{10,6},{14,10},{7,3},{... | collective-permute-start | bytes 92168 | tf_op jit(solution)/shard_map/ppermute | solution.py:28
  41.0 3.9 %collective-permute-start.3 = (f32[5,8,1,192]{3,1,2,0:T(8,128)S(1)}, f32[5,8,1,192]{3,1,2,0:T(8,128)S(1)}, u32[]{:S(2)}, u32[]{:S(2)}) collective-permute-start(f32[5,8,1,192]{3,1,2,0:T(8,128)S(1)} %get-tuple-element.14), channel_id=1, source_target_pairs={{0,4},{4,8},{8,12},{1,5},{5,9},{9,13},{2,6},{6,10},{10,14},{3,7},{... | collective-permute-start | bytes 92168 | tf_op jit(solution)/shard_map/ppermute | solution.py:27
  45.3 13.6 %collective-permute-start.5 = (f32[5,8,14,1]{3,1,2,0:T(8,128)S(1)}, f32[5,8,14,1]{3,1,2,0:T(8,128)}, u32[]{:S(2)}, u32[]{:S(2)}) collective-permute-start(f32[5,8,14,1]{3,1,2,0:T(8,128)S(1)} %get-tuple-element.19), channel_id=1, source_target_pairs={{0,1},{1,2},{2,3},{4,5},{5,6},{6,7},{8,9},{9,10},{10,11},{12,13},{... | collective-permute-start | bytes 6728 | tf_op jit(solution)/shard_map/ppermute | solution.py:27
  49.5 11.6 %collective-permute-start.4 = (f32[5,8,14,1]{3,1,2,0:T(8,128)S(1)}, f32[5,8,14,1]{3,1,2,0:T(8,128)}, u32[]{:S(2)}, u32[]{:S(2)}) collective-permute-start(f32[5,8,14,1]{3,1,2,0:T(8,128)S(1)} %get-tuple-element.18), channel_id=1, source_target_pairs={{1,0},{2,1},{3,2},{5,4},{6,5},{7,6},{9,8},{10,9},{11,10},{13,12},{... | collective-permute-start | bytes 6728 | tf_op jit(solution)/shard_map/ppermute | solution.py:28
  51.0 7.7 %copy-start.11 = (f32[4,15,32]{2,0,1:T(4,128)S(1)}, f32[4,15,32]{2,0,1:T(4,128)}, u32[]{:S(2)}) copy-start(f32[4,15,32]{2,0,1:T(4,128)} %param.15) | copy-start | bytes 23044
  61.0 3.6 %copy-start.4 = (f32[6,12,192]{2,1,0:T(8,128)S(1)}, f32[6,12,192]{2,1,0:T(8,128)}, u32[]{:S(2)}) copy-start(f32[6,12,192]{2,1,0:T(8,128)} %add_add_fusion) | copy-start | bytes 165892
  67.9 6.5 %collective-permute-start.6 = (f32[5,1,12,192]{3,1,2,0:T(1,128)S(1)}, f32[5,1,12,192]{3,1,2,0:T(1,128)S(1)}, u32[]{:S(2)}, u32[]{:S(2)}) collective-permute-start(f32[5,1,12,192]{3,1,2,0:T(1,128)S(1)} %get-tuple-element.21), channel_id=1, source_target_pairs={{16,0},{17,1},{18,2},{19,3},{20,4},{21,5},{22,6},{23,7},{24,8},{25... | collective-permute-start | bytes 138248 | tf_op jit(solution)/shard_map/ppermute | solution.py:28
  69.2 6.4 %collective-permute-start.7 = (f32[5,1,12,192]{3,1,2,0:T(1,128)S(1)}, f32[5,1,12,192]{3,1,2,0:T(1,128)S(1)}, u32[]{:S(2)}, u32[]{:S(2)}) collective-permute-start(f32[5,1,12,192]{3,1,2,0:T(1,128)S(1)} %get-tuple-element.20), channel_id=1, source_target_pairs={{0,16},{1,17},{2,18},{3,19},{4,20},{5,21},{6,22},{7,23},{8,24},{9,... | collective-permute-start | bytes 138248 | tf_op jit(solution)/shard_map/ppermute | solution.py:27
  75.6 5.4 %collective-permute-start.8 = (f32[5,8,1,192]{3,1,2,0:T(8,128)S(1)}, f32[5,8,1,192]{3,1,2,0:T(8,128)S(1)}, u32[]{:S(2)}, u32[]{:S(2)}) collective-permute-start(f32[5,8,1,192]{3,1,2,0:T(8,128)S(1)} %get-tuple-element.13), channel_id=1, source_target_pairs={{4,0},{8,4},{12,8},{5,1},{9,5},{13,9},{6,2},{10,6},{14,10},{7,3},{... | collective-permute-start | bytes 92168 | tf_op jit(solution)/shard_map/ppermute | solution.py:28
  76.9 4.1 %collective-permute-start.9 = (f32[5,8,1,192]{3,1,2,0:T(8,128)S(1)}, f32[5,8,1,192]{3,1,2,0:T(8,128)S(1)}, u32[]{:S(2)}, u32[]{:S(2)}) collective-permute-start(f32[5,8,1,192]{3,1,2,0:T(8,128)S(1)} %get-tuple-element.12), channel_id=1, source_target_pairs={{0,4},{4,8},{8,12},{1,5},{5,9},{9,13},{2,6},{6,10},{10,14},{3,7},{... | collective-permute-start | bytes 92168 | tf_op jit(solution)/shard_map/ppermute | solution.py:27
  81.4 7.4 %collective-permute-start.11 = (f32[5,8,14,1]{3,1,2,0:T(8,128)S(1)}, f32[5,8,14,1]{3,1,2,0:T(8,128)S(1)}, u32[]{:S(2)}, u32[]{:S(2)}) collective-permute-start(f32[5,8,14,1]{3,1,2,0:T(8,128)S(1)} %get-tuple-element.17), channel_id=1, source_target_pairs={{0,1},{1,2},{2,3},{4,5},{5,6},{6,7},{8,9},{9,10},{10,11},{12,13},{... | collective-permute-start | bytes 6728 | tf_op jit(solution)/shard_map/ppermute | solution.py:27
  83.8 9.7 %collective-permute-start.10 = (f32[5,8,14,1]{3,1,2,0:T(8,128)S(1)}, f32[5,8,14,1]{3,1,2,0:T(8,128)S(1)}, u32[]{:S(2)}, u32[]{:S(2)}) collective-permute-start(f32[5,8,14,1]{3,1,2,0:T(8,128)S(1)} %get-tuple-element.16), channel_id=1, source_target_pairs={{1,0},{2,1},{3,2},{5,4},{6,5},{7,6},{9,8},{10,9},{11,10},{13,12},{... | collective-permute-start | bytes 6728 | tf_op jit(solution)/shard_map/ppermute | solution.py:28
  97.4 17.9 %copy-start.5 = (f32[64,128]{1,0:T(8,128)S(1)}, f32[64,128]{1,0:T(8,128)}, u32[]{:S(2)}) copy-start(f32[64,128]{1,0:T(8,128)} %get-tuple-element.27) | copy-start | bytes 98308
  97.4 17.9 %copy-start.6 = (f32[64,128]{1,0:T(8,128)S(1)}, f32[64,128]{1,0:T(8,128)}, u32[]{:S(2)}) copy-start(f32[64,128]{1,0:T(8,128)} %get-tuple-element.28) | copy-start | bytes 98308
  97.4 17.9 %copy-start.7 = (f32[64,128]{1,0:T(8,128)S(1)}, f32[64,128]{1,0:T(8,128)}, u32[]{:S(2)}) copy-start(f32[64,128]{1,0:T(8,128)} %get-tuple-element.30) | copy-start | bytes 98308
  97.4 17.9 %copy-start.8 = (f32[64,128]{1,0:T(8,128)S(1)}, f32[64,128]{1,0:T(8,128)}, u32[]{:S(2)}) copy-start(f32[64,128]{1,0:T(8,128)} %get-tuple-element.24) | copy-start | bytes 98308
  97.5 17.9 %copy-start.9 = (f32[64,128]{1,0:T(8,128)S(1)}, f32[64,128]{1,0:T(8,128)}, u32[]{:S(2)}) copy-start(f32[64,128]{1,0:T(8,128)} %get-tuple-element.25) | copy-start | bytes 98308
  97.5 17.9 %copy-start.10 = (f32[64,128]{1,0:T(8,128)S(1)}, f32[64,128]{1,0:T(8,128)}, u32[]{:S(2)}) copy-start(f32[64,128]{1,0:T(8,128)} %get-tuple-element.26) | copy-start | bytes 98308
where the time goes:
time: 144 us
  blocking collectives  53.4 us (37%)
  starting transfers between devices  30.3 us (21%)
  local copies, waits for them, and re-layouts  19.8 us (14%)
  matrix products  17.4 us (12%)
  waiting for transfers between devices  11.9 us (8%)
  other arithmetic  9.8 us (7%)
    psum x1, blocking collectives, on_device(): spectra = lax.psum(partial_sums, ('flow', 'col'))  25.7 us
    ppermute x6, starting transfers between devices, with_halo(): before = lax.ppermute(last, axis, up)  22.3 us
    all_gather x1, blocking collectives, on_device(): lax.all_gather(surface_samples, 'row', axis=2, tiled=True)  14.4 us
    all_gather x1, blocking collectives, on_device(): lax.all_gather(panel_points, 'row', axis=1, tiled=True)  13.2 us
    dot_general x12, matrix products, contract_small(): result = jnp.einsum('...p,qp->...q', blocked, matrix, precision=HIGH)  11.6 us
    ppermute x6, starting transfers between devices, with_halo(): after = lax.ppermute(first, axis, down)  7.92 us
    ppermute x6, waiting for transfers between devices, with_halo(): after = lax.ppermute(first, axis, down)  6.94 us
    mul x1, other arithmetic, on_device(): wide_back = jnp.kron(identity, eigen_bases[2])  4.95 us
  transfers between devices with their start and end apart: 12, of which 5 were waited for; matrix products, arithmetic and copies ran while one was open for 20% of the time, Pallas kernels for 0%

commit v1 on v0

v1 whole, which is shorter than its diff:
```python
import functools
import math

import jax
import jax.numpy as jnp
from jax import lax
from jax.experimental import pallas as pl
from jax.experimental.pallas import tpu as pltpu
from jax.sharding import PartitionSpec as P

N = 6
SWEEPS = 2
NT = 16
NF = 16
OMEGA = 0.8
TAU = 0.5
KMAX = 2.0
BLK = 256
HIGH = lax.Precision.HIGHEST
MESH = pl.DeviceIdType.MESH
F32 = jnp.float32
NN = (((1,), (0,)), ((), ()))
NTD = (((1,), (1,)), ((), ()))


def ddot(a, b, dims=NN):
    return lax.dot_general(a, b, dims, precision=HIGH, preferred_element_type=F32)


def split(a):
    hi = a.astype(jnp.bfloat16)
    return hi, (a - hi.astype(F32)).astype(jnp.bfloat16)


def dot3(a, b):
    f = functools.partial(lax.dot_general, dimension_numbers=NN, preferred_element_type=F32)
    return f(a[0], b[0]) + (f(a[0], b[1]) + f(a[1], b[0]))


def rows_of(n):
    return lax.broadcasted_iota(jnp.int32, (n, 1), 0).astype(F32)


def cols_of(n):
    return lax.broadcasted_iota(jnp.int32, (1, n), 1).astype(F32)


def divmod_of(v, n):
    q = jnp.floor((v + 0.5) * (1.0 / n))
    return q, v - n * q


def where01(cond):
    return jnp.where(cond, 1.0, 0.0).astype(F32)


def pick(m, r, c, transposed=False):
    left = ddot(where01(r == cols_of(N)), m, NTD if transposed else NN)
    return ddot(left, where01(rows_of(N) == c))


def kernel(
    sizes, f_hbm, u_hbm, lam_ref, bases_ref, vals_ref, obs_ref, pts_ref, hist_ref,
    out_hbm, spec_ref,
    f_in, u_in, out_buf, u_s, f_s, r_s, trace_s, zsend_s, halo_r, z_r,
    pan_s, pan_r, new_s, new_r, er_s, ei_s, part_s, part_r,
    local_sem, hs_sem, hr_sem, ps_sem, pr_sem, ns_sem, nr_sem, ss_sem, sr_sem,
):
    n_flow, n_col, n_row, comps, nx, ny, nz, pan, n_obs = sizes
    ey = ny // N
    nh = nx * ny
    own_obs = n_obs // n_row
    flow, col, row = (lax.axis_index(a) for a in ("flow", "col", "row"))
    n_fc = n_flow * n_col
    fc = flow * n_col + col

    def fc_peer(d):
        t = lax.rem(fc + d, n_fc)
        return (lax.div(t, n_col), lax.rem(t, n_col), row)

    def row_peer(d):
        return (flow, col, lax.rem(row + d, n_row))

    def each_fc(body):
        if n_fc <= 16:
            for d in range(1, n_fc):
                body(d)
        else:
            lax.fori_loop(1, n_fc, lambda d, c: (body(d), c)[1], 0)

    u_copy = pltpu.make_async_copy(u_hbm, u_in, local_sem.at[0])
    f_copy = pltpu.make_async_copy(f_hbm, f_in, local_sem.at[1])
    u_copy.start()
    f_copy.start()
    halo_r[...] = jnp.zeros(halo_r.shape, F32)
    z_r[...] = jnp.zeros(z_r.shape, F32)
    barrier = pltpu.get_barrier_semaphore()
    each_fc(lambda d: pl.semaphore_signal(barrier, inc=1, device_id=fc_peer(d), device_id_type=MESH))
    for d in range(1, n_row):
        pl.semaphore_signal(barrier, inc=1, device_id=row_peer(d), device_id_type=MESH)

    place = where01(cols_of(128) == rows_of(pan) + (row * pan).astype(F32))
    pan_s[...] = jnp.zeros(pan_s.shape, F32)
    for c in range(4):
        pan_s[c * 16 : c * 16 + NT - 1, :] = ddot(hist_ref[c], place)
    pan_s[64:67, :] = ddot(pts_ref[...], place)

    sx, sy, sz = bases_ref[0], bases_ref[1], bases_ref[2]

    def ends(m, labels, is_row):
        if is_row:
            one = where01(rows_of(N) == labels)
            both = ddot(m, one)
            return both[0:1], both[N - 1 : N]
        one = where01(labels == cols_of(N))
        return (
            jnp.sum(one * m[0:1], axis=1, keepdims=True),
            jnp.sum(one * m[N - 1 : N], axis=1, keepdims=True),
        )

    hr = rows_of(nh)
    hc = cols_of(nh)
    ir, yr = divmod_of(hr, ny)
    er, jr = divmod_of(yr, N)
    ic, yc = divmod_of(hc, ny)
    ec, jc = divmod_of(yc, N)
    x0r, x5r = ends(sx, ic, True)
    y0r, y5r = ends(sy, jc, True)
    x0c, x5c = ends(sx, ir, False)
    y0c, y5c = ends(sy, jr, False)

    def spread(count, period):
        return divmod_of(count, period)

    nc, myc = divmod_of(cols_of(nx * 16), 16)
    mec, mjc = divmod_of(myc, N)
    nr, myr = divmod_of(rows_of(nx * 16), 16)
    mer, mjr = divmod_of(myr, N)
    a_fwd = pick(sx, ir, nc, True) * pick(sy, jr, mjc, True) * where01((er == mec) & (myc < ny))
    zqr, zkr = divmod_of(rows_of(BLK), N)
    zqc, zkc = divmod_of(cols_of(BLK), N)
    zqn, zkn = divmod_of(rows_of(nz), N)
    z_fwd = pick(sz, zkn, zkc) * where01(zqn == zqc)
    a_fwd = split(a_fwd)
    z_fwd = split(z_fwd)

    z0r, z5r = ends(sz, zkc, True)
    z0c, z5c = ends(sz, zkr, False)
    lane = cols_of(BLK)
    ez = nz // N
    inside = lane < nz
    kz = where01((zqr == zqc + 1) & inside & (rows_of(BLK) < nz)) * z0c * z5r
    kz = kz + where01((zqr == zqc - 1) & inside) * z5c * z0r
    first_lane = (lane >= nz) & (lane < nz + comps)
    last_lane = (lane >= nz + 8) & (lane < nz + 8 + comps)
    kz = kz + where01((zqr == 0) & first_lane) * z0c + where01((zqr == ez - 1) & last_lane) * z5c
    kz = split(kz)

    ky = where01(ir == ic) * (
        where01(ec == er + 1) * y5c * y0r + where01(ec == er - 1) * y0c * y5r
    )
    t16, t8 = rows_of(16), rows_of(8)
    mxy = jnp.concatenate(
        [
            ky,
            where01(t16 == yc) * x0r,
            where01(t16 == yc) * x5r,
            where01((t8 == ic) & (ec == 0)) * y0r,
            where01((t8 == ic) & (ec == ey - 1)) * y5r,
        ],
        axis=0,
    )
    mxy = split(mxy)
    hl = cols_of(48)
    inj = where01(hl == yr) * x5c + where01(hl == yr + 16) * x0c
    inj = inj + where01((hl == ir + 32) & (er == ey - 1)) * y5c
    inj = inj + where01((hl == ir + 40) & (er == 0)) * y0c
    inj = split(inj)
    zin5 = jnp.where(zqc == ez - 1, z5r, 0.0)[:, 128:256]
    zin0 = jnp.where(zqc == 0, z0r, 0.0)[:, 0:128]

    pl.semaphore_wait(barrier, (n_fc - 1) + (n_row - 1))

    def pan_copy(d):
        return pltpu.make_async_remote_copy(
            src_ref=pan_s, dst_ref=pan_r.at[d], send_sem=ps_sem.at[d], recv_sem=pr_sem.at[d],
            device_id=row_peer(d), device_id_type=MESH)

    def new_copy(d):
        return pltpu.make_async_remote_copy(
            src_ref=new_s, dst_ref=new_r.at[d], send_sem=ns_sem.at[d], recv_sem=nr_sem.at[d],
            device_id=row_peer(d), device_id_type=MESH)

    def part_copy(d):
        return pltpu.make_async_remote_copy(
            src_ref=part_s, dst_ref=part_r.at[fc], send_sem=ss_sem.at[d], recv_sem=sr_sem.at[d],
            device_id=fc_peer(d), device_id_type=MESH)

    def part_wait(d):
        src = lax.rem(fc + (n_fc - d), n_fc)
        pltpu.make_async_remote_copy(
            src_ref=part_s, dst_ref=part_r.at[src], send_sem=ss_sem.at[d], recv_sem=sr_sem.at[d],
            device_id=fc_peer(d), device_id_type=MESH).wait_recv()

    def faces(s):
        def copy(k, src, dst, where):
            return pltpu.make_async_remote_copy(
                src_ref=src, dst_ref=dst, send_sem=hs_sem.at[s, k], recv_sem=hr_sem.at[s, k],
                device_id=where, device_id_type=MESH)

        def rows(buf, a, n):
            return buf.at[s, pl.ds(a, n), :]

        return (
            (flow > 0, flow < n_flow - 1, copy(0, rows(trace_s, 0, 16), rows(halo_r, 0, 16), (flow - 1, col, row))),
            (flow < n_flow - 1, flow > 0, copy(1, rows(trace_s, 16, 16), rows(halo_r, 16, 16), (flow + 1, col, row))),
            (col > 0, col < n_col - 1, copy(2, rows(trace_s, 32, 8), rows(halo_r, 32, 8), (flow, col - 1, row))),
            (col < n_col - 1, col > 0, copy(3, rows(trace_s, 40, 8), rows(halo_r, 40, 8), (flow, col + 1, row))),
            (row > 0, row < n_row - 1, copy(4, zsend_s.at[s], z_r.at[s, 0], (flow, col, row - 1))),
            (row < n_row - 1, row > 0, copy(5, zsend_s.at[s], z_r.at[s, 1], (flow, col, row + 1))),
        )

    def forward(ref):
        parts = []
        for c in range(comps):
            fill = jnp.zeros((16 - ny, nz), F32)
            x = jnp.concatenate([p for i in range(nx) for p in (ref[c, i], fill)], axis=0)
            y = dot3(split(x), z_fwd)
            parts.append(dot3(a_fwd, split(y)))
        return parts

    def couple(parts, s):
        acc = None
        inner = []
        for c in range(comps):
            u = split(parts[c])
            w = dot3(u, kz)
            t = dot3(mxy, u)
            trace_s[s, :, c * BLK : (c + 1) * BLK] = t[nh : nh + 48]
            lanes = cols_of(128)
            keep = (lanes == nz - 128 + c) | (lanes == nz - 120 + c)
            piece = jnp.where(keep, w[:, 128:256], 0.0)
            acc = piece if acc is None else acc + piece
            inner.append(w + t[:nh])
        zsend_s[s] = acc
        for sends, _, copy in faces(s):
            pl.when(sends)(copy.start)
        return inner

    def finish(s):
        for _, receives, copy in faces(s):
            pl.when(receives)(copy.wait_recv)

    def update(parts, inner, s):
        zn, zp = z_r[s, 0], z_r[s, 1]
        r = r_s[...]
        new = []
        for c in range(comps):
            add = dot3(inj, split(halo_r[s, :, c * BLK : (c + 1) * BLK]))
            zlo = zp[:, nz - 120 + c : nz - 119 + c] * zin0
            zhi = zn[:, nz - 128 + c : nz - 127 + c] * zin5
            total = inner[c] + add + jnp.concatenate([zlo, zhi], axis=1)
            new.append((1.0 - OMEGA) * parts[c] + r * (f_s[c] + TAU * total))
        return new

    u_copy.wait()
    state = forward(u_in)
    inner = couple(state, 0)
    for c in range(comps):
        u_s[c] = state[c]
    for d in range(1, n_row):
        pan_copy(d).start()

    f_copy.wait()
    for c, part in enumerate(forward(f_in)):
        f_s[c] = part
    lam = ddot(ddot(where01(er == cols_of(ey)), lam_ref[0]), where01(rows_of(ez) == zqc))
    onx = jnp.sum(where01(ir == cols_of(N)) * vals_ref[0:1, :], axis=1, keepdims=True)
    ony = jnp.sum(where01(jr == cols_of(N)) * vals_ref[1:2, :], axis=1, keepdims=True)
    onz = ddot(vals_ref[...], where01(rows_of(N) == zkc))[2:3]
    r_s[...] = jnp.where(inside, OMEGA / jnp.where(inside, lam + onx + ony + onz, 1.0), 0.0)

    finish(0)
    state = update([u_s[c] for c in range(comps)], inner, 0)
    inner = couple(state, 1)
    for c in range(comps):
        u_s[c] = state[c]

    for d in range(1, n_row):
        pan_copy(d).wait_recv()
    panels = pan_s[...]
    for d in range(1, n_row):
        panels = panels + pan_r[d]
    own = where01(cols_of(n_obs) == rows_of(own_obs) + (row * own_obs).astype(F32))
    mine = ddot(own, obs_ref[...], NTD)
    dx, dy, dz = (mine[:, a : a + 1] - panels[64 + a : 65 + a, :] for a in range(3))
    r2 = dx * dx + dy * dy + dz * dz
    radius = jnp.sqrt(r2)
    inv = 1.0 / radius
    dx, dy, dz = dx * inv, dy * inv, dz * inv
    amp = inv * (1.0 / (4.0 * math.pi))
    step = KMAX / NF
    ar, ai = jnp.cos(radius * (0.5 * step)), -jnp.sin(radius * (0.5 * step))
    sr, si = ar * ar - ai * ai, 2.0 * ar * ai
    ar, ai = ar * amp, ai * amp
    angle = (rows_of(NF) + 0.5) * (math.pi / NF) * cols_of(NT)
    cos_t, sin_t = jnp.cos(angle), -jnp.sin(angle)
    both_t = jnp.concatenate([cos_t, sin_t], axis=0)
    q = [ddot(both_t, panels[c * 16 : (c + 1) * 16, :]) for c in range(4)]
    lane128 = lax.broadcasted_iota(jnp.int32, (1, 128), 1)
    total = jnp.zeros((own_obs, 128), F32)
    for f in range(NF):
        k = step * (f + 0.5)
        er_s[f], ei_s[f] = ar, ai
        re, im = [x[f : f + 1] for x in q], [x[NF + f : NF + f + 1] for x in q]
        d_re = dx * re[1] + dy * re[2] + dz * re[3]
        d_im = dx * im[1] + dy * im[2] + dz * im[3]
        t_re = d_re * inv - k * (im[0] + d_im)
        t_im = d_im * inv + k * (re[0] + d_re)
        s_re = jnp.sum(ar * t_re - ai * t_im, axis=1, keepdims=True)
        s_im = jnp.sum(ar * t_im + ai * t_re, axis=1, keepdims=True)
        total = jnp.where(lane128 == f, s_re, total)
        total = jnp.where(lane128 == NF + f, s_im, total)
        if f < NF - 1:
            ar, ai = ar * sr - ai * si, ar * si + ai * sr

    a_back = pick(sx, nr, ic) * pick(sy, mjr, jc) * where01((mer == ec) & (myr < ny))
    a_back = split(a_back)
    zq_own, zk_own = divmod_of(cols_of(nz), N)
    z_back = split(pick(sz, zkr, zk_own, True) * where01(zqr == zq_own))
    zs = cols_of(128) - (row * pan).astype(F32)
    sq, sk = divmod_of(zs, N)
    z_new = pick(sz, zkr, sk, True) * where01((zqr == sq) & (zs >= 0) & (zs < pan))
    z_new = split(z_new)
    last_re = jnp.sum(jnp.where(cols_of(NT) == NT - 1, both_t, 0.0), axis=1, keepdims=True)

    finish(1)
    state = update([u_s[c] for c in range(comps)], inner, 1)
    corner = (a_back[0][0:16], a_back[1][0:16])
    eight = rows_of(8)
    corners = jnp.zeros((8, BLK), F32)
    halves = [split(s) for s in state]
    for c in range(4):
        corners = jnp.where(eight == c, dot3(corner, halves[c])[0:1], corners)
    new_s[...] = dot3(split(corners), z_new)
    for d in range(1, n_row):
        new_copy(d).start()

    for c in range(comps):
        w = dot3(halves[c], z_back)
        nodes = dot3(a_back, split(w))
        for i in range(nx):
            out_buf[c, i] = nodes[i * 16 : i * 16 + ny]
    out_copy = pltpu.make_async_copy(out_buf, out_hbm, local_sem.at[2])
    out_copy.start()

    for d in range(1, n_row):
        new_copy(d).wait_recv()
    newest = new_s[...]
    for d in range(1, n_row):
        newest = newest + new_r[d]
    along = dx * newest[1:2] + dy * newest[2:3] + dz * newest[3:4]
    a_val = newest[0:1] + along
    b_val = along * inv
    fresh = jnp.zeros((own_obs, 128), F32)
    for f in range(NF):
        k = step * (f + 0.5)
        ka = k * a_val
        gr, gi = er_s[f], ei_s[f]
        s_re = jnp.sum(gr * b_val - gi * ka, axis=1, keepdims=True)
        s_im = jnp.sum(gr * ka + gi * b_val, axis=1, keepdims=True)
        fresh = jnp.where(lane128 == f, s_re, fresh)
        fresh = jnp.where(lane128 == NF + f, s_im, fresh)
    turned = jnp.concatenate([fresh, total], axis=0).T
    fr, fi = turned[0:NF], turned[NF : 2 * NF]
    c15, s15 = last_re[0:NF], last_re[NF : 2 * NF]
    now_re = c15 * fr - s15 * fi
    now_im = c15 * fi + s15 * fr
    part_s[0:NF, :] = now_re + pltpu.roll(fr, own_obs, 1)
    part_s[NF : 2 * NF, :] = now_im + pltpu.roll(fi, own_obs, 1)
    part_r[fc] = part_s[...]
    each_fc(lambda d: part_copy(d).start())
    each_fc(part_wait)
    if n_fc <= 16:
        spectra = part_r[0]
        for d in range(1, n_fc):
            spectra = spectra + part_r[d]
    else:
        spectra = lax.fori_loop(1, n_fc, lambda d, acc: acc + part_r[d], part_r[0])
    spec_ref[0] = spectra[0:NF, :own_obs]
    spec_ref[1] = spectra[NF : 2 * NF, :own_obs]

    for s in range(SWEEPS):
        for sends, _, copy in faces(s):
            pl.when(sends)(copy.wait_send)
    for d in range(1, n_row):
        pan_copy(d).wait_send()
        new_copy(d).wait_send()
    each_fc(lambda d: part_copy(d).wait_send())
    out_copy.wait()


def on_device(forcing, previous, shift, bases, values, observers, points, history):
    n_flow, n_col, n_row = (lax.axis_size(a) for a in ("flow", "col", "row"))
    comps, nx, ny, nz = forcing.shape
    n_fc = n_flow * n_col
    pan = points.shape[1]
    n_obs = observers.shape[1]
    own_obs = n_obs // n_row
    nh = nx * ny
    sizes = (n_flow, n_col, n_row, comps, nx, ny, nz, pan, n_obs)
    vmem = pl.BlockSpec(memory_space=pltpu.VMEM)
    hbm = pl.BlockSpec(memory_space=pl.ANY)
    dma = pltpu.SemaphoreType.DMA
    return pl.pallas_call(
        functools.partial(kernel, sizes),
        out_shape=(
            jax.ShapeDtypeStruct(forcing.shape, F32),
            jax.ShapeDtypeStruct((2, NF, own_obs), F32),
        ),
        in_specs=[hbm, hbm] + [vmem] * 6,
        out_specs=(hbm, vmem),
        scratch_shapes=[
            pltpu.VMEM((comps, nx, ny, nz), F32),
            pltpu.VMEM((comps, nx, ny, nz), F32),
            pltpu.VMEM((comps, nx, ny, nz), F32),
            pltpu.VMEM((comps, nh, BLK), F32),
            pltpu.VMEM((comps, nh, BLK), F32),
            pltpu.VMEM((nh, BLK), F32),
            pltpu.VMEM((SWEEPS, 48, comps * BLK), F32),
            pltpu.VMEM((SWEEPS, nh, 128), F32),
            pltpu.VMEM((SWEEPS, 48, comps * BLK), F32),
            pltpu.VMEM((SWEEPS, 2, nh, 128), F32),
            pltpu.VMEM((72, 128), F32),
            pltpu.VMEM((n_row, 72, 128), F32),
            pltpu.VMEM((8, 128), F32),
            pltpu.VMEM((n_row, 8, 128), F32),
            pltpu.VMEM((NF, own_obs, 128), F32),
            pltpu.VMEM((NF, own_obs, 128), F32),
            pltpu.VMEM((2 * NF, 128), F32),
            pltpu.VMEM((n_fc, 2 * NF, 128), F32),
            dma((3,)),
            dma((SWEEPS, 6)),
            dma((SWEEPS, 6)),
            dma((n_row,)),
            dma((n_row,)),
            dma((n_row,)),
            dma((n_row,)),
            dma((n_fc,)),
            dma((n_fc,)),
        ],
        compiler_params=pltpu.CompilerParams(
            collective_id=0, has_side_effects=True, vmem_limit_bytes=48 * 1024 * 1024
        ),
    )(forcing, previous, shift, bases, values, observers, points, history)


def solution(mesh):
    return jax.shard_map(
        on_device,
        mesh=mesh,
        in_specs=(
            P(None, "flow", "col", "row"),
            P(None, "flow", "col", "row"),
            P("flow", "col", "row"),
            P(),
            P(),
            P(),
            P(None, ("flow", "col", "row")),
            P(None, None, ("flow", "col", "row")),
        ),
        out_specs=(P(None, "flow", "col", "row"), P(None, None, "row")),
        check_vma=False,
    )
```

time: 144 us -> 29 us (0.20)
  blocking collectives: 53.4 us -> 0 us
  starting transfers between devices: 30.3 us -> 0 us
  Pallas kernels: 0 us -> 23.8 us
  matrix products: 17.4 us -> 0 us
  local copies, waits for them, and re-layouts: 19.8 us -> 4.25 us
  waiting for transfers between devices: 11.9 us -> 0 us
  other arithmetic: 9.8 us -> 0 us
    ppermute x12 -> x0, starting transfers between devices: 30.3 us -> none  [the longest x6 22.3 us: with_halo(): before = lax.ppermute(last, axis, up)]
    all_gather x2 -> x0, blocking collectives: 27.7 us -> none  [the longest x1 14.4 us: on_device(): lax.all_gather(surface_samples, 'row', axis=2, tiled=True)]
    psum x1 -> x0, blocking collectives: 25.7 us -> none  [on_device(): spectra = lax.psum(partial_sums, ('flow', 'col'))]
    pallas_call x0 -> x1, Pallas kernels: none -> 23.8 us  [on_device(): pl.pallas_call(functools.partial(kernel, sizes), out_shape=(jax.ShapeDtyp...]
    dot_general x23 -> x0, matrix products: 17.4 us -> none  [the longest x12 11.6 us: contract_small(): result = jnp.einsum('...p,qp->...q', blocked, matrix, precision=HIGH)]
    mul x6 -> x0, local copies, waits for them, and re-layouts: 13.1 us -> none  [the longest x1 3.93 us: on_device(): wide_stiff = jnp.kron(identity, stiffness[2])]
    ppermute x12 -> x0, waiting for transfers between devices: 11.9 us -> none  [the longest x6 6.94 us: with_halo(): after = lax.ppermute(first, axis, down)]
    mul x1 -> x0, other arithmetic: 4.95 us -> none  [on_device(): wide_back = jnp.kron(identity, eigen_bases[2])]
  transfers between devices with their start and end apart: 12 -> 0, of which waited for: 5 -> 0; matrix products, arithmetic and copies ran while one was open for 20% -> 0% of each run, Pallas kernels for 0% -> 0%
where the time goes in v1:
time: 29 us; the launch traced here: 28.7 us
  Pallas kernels  23.8 us (82%)
  local copies, waits for them, and re-layouts  4.25 us (15%)
  between operations  0.72 us (2%)
    pallas_call x1, Pallas kernels, on_device(): pl.pallas_call(functools.partial(kernel, sizes), out_shape=(jax.ShapeDtyp...  23.8 us
    unnamed x17, local copies, waits for them, and re-layouts  4.25 us

profile of v1, /device:TPU:0, one launch (start us, length us, event | category | flops | bytes accessed | tf_op | source)
XLA Modules:
  0.0 28.7 jit_solution(16769125160576121727)
XLA Ops:
  0.6 0.0 copy-start.5
  0.6 0.0 copy-start.3
  0.7 0.0 copy-start.4
  0.7 0.0 copy-start.2
  0.7 0.0 copy-start.6
  0.7 0.8 %copy.10.hist_ref = f32[4,15,32]{2,1,0:T(8,128)S(1)} copy(f32[4,15,32]{2,0,1:T(4,128)} %param.15) | data formatting | bytes 15360 | tf_op args[7]
  1.5 0.0 copy-done.5
  1.5 0.0 copy-done.3
  1.5 0.0 copy-done.4
  1.5 0.0 copy-done.2
  1.5 0.0 copy-done.6
  1.5 0.0 copy-start
  1.5 1.0 %copy-done = f32[5,6,12,192]{3,2,1,0:T(8,128)S(1)} copy-done((f32[5,6,12,192]{3,2,1,0:T(8,128)S(1)}, f32[5,6,12,192]{3,2,1,0:T(8,128)}, u32[]{:S(2)}) %copy-start) | copy-done | bytes 276504
  2.5 0.0 copy-start.1
  2.5 1.0 %copy-done.1 = f32[5,6,12,192]{3,2,1,0:T(8,128)S(1)} copy-done((f32[5,6,12,192]{3,2,1,0:T(8,128)S(1)}, f32[5,6,12,192]{3,2,1,0:T(8,128)}, u32[]{:S(2)}) %copy-start.1) | copy-done | bytes 276504
  3.6 23.8 %shard_map.95 = (f32[5,6,12,192]{3,2,1,0:T(8,128)S(1)}, f32[2,16,64]{2,1,0:T(8,128)S(1)}) custom-call(f32[5,6,12,192]{3,2,1,0:T(8,128)S(1)} %copy-done, f32[5,6,12,192]{3,2,1,0:T(8,128)S(1)} %copy-done.1, f32[1,2,32]{2,1,0:T(2,128)S(1)} %copy-done.6, f32[3,6,6]{2,1,0:T(8,128)S(1)} %copy-done.2, f32[3,6]{1,0:T(4,128)S(1)} %copy-done.4, ...), custom_call_target="tpu_custom_call" | custom-call | tf_op jit(solution)/shard_map/pallas_call | solution.py:415
  27.3 0.8 %copy.13 = f32[5,6,12,192]{3,2,1,0:T(8,128)} copy(f32[5,6,12,192]{3,2,1,0:T(8,128)S(1)} %get-tuple-element.4) | data formatting | bytes 552960
  28.1 0.6 %copy.14 = f32[2,16,64]{2,1,0:T(8,128)} copy(f32[2,16,64]{2,1,0:T(8,128)S(1)} %get-tuple-element.5) | data formatting | bytes 16384
Async XLA Ops:
  0.6 0.8 %copy-start.5 = (f32[3,32]{1,0:T(4,128)S(1)}, f32[3,32]{1,0:T(4,128)}, u32[]{:S(2)}) copy-start(f32[3,32]{1,0:T(4,128)} %pts_ref.1) | copy-start | bytes 1156
  0.6 0.8 %copy-start.3 = (f32[3,256]{1,0:T(4,128)S(1)}, f32[3,256]{1,0:T(4,128)}, u32[]{:S(2)}) copy-start(f32[3,256]{1,0:T(4,128)} %obs_ref.1) | copy-start | bytes 9220
  0.7 0.8 %copy-start.4 = (f32[3,6]{1,0:T(4,128)S(1)}, f32[3,6]{1,0:T(4,128)}, u32[]{:S(2)}) copy-start(f32[3,6]{1,0:T(4,128)} %vals_ref.1) | copy-start | bytes 220
  0.7 0.8 %copy-start.2 = (f32[3,6,6]{2,1,0:T(8,128)S(1)}, f32[3,6,6]{2,1,0:T(8,128)}, u32[]{:S(2)}) copy-start(f32[3,6,6]{2,1,0:T(8,128)} %bases_ref.1) | copy-start | bytes 1300
  0.7 0.8 %copy-start.6 = (f32[1,2,32]{2,1,0:T(2,128)S(1)}, f32[1,2,32]{2,1,0:T(2,128)}, u32[]{:S(2)}) copy-start(f32[1,2,32]{2,1,0:T(2,128)} %lam_ref.1) | copy-start | bytes 772
  1.5 1.0 %copy-start = (f32[5,6,12,192]{3,2,1,0:T(8,128)S(1)}, f32[5,6,12,192]{3,2,1,0:T(8,128)}, u32[]{:S(2)}) copy-start(f32[5,6,12,192]{3,2,1,0:T(8,128)} %f_hbm.1) | copy-start | bytes 829444
  2.5 1.0 %copy-start.1 = (f32[5,6,12,192]{3,2,1,0:T(8,128)S(1)}, f32[5,6,12,192]{3,2,1,0:T(8,128)}, u32[]{:S(2)}) copy-start(f32[5,6,12,192]{3,2,1,0:T(8,128)} %u_hbm.1) | copy-start | bytes 829444

commit v2 on v1

v2 whole, which is shorter than its diff:
```python
import functools
import math

import jax
import jax.numpy as jnp
from jax import lax
from jax.experimental import pallas as pl
from jax.experimental.pallas import tpu as pltpu
from jax.sharding import PartitionSpec as P

N = 6
SWEEPS = 2
NT = 16
NF = 16
OMEGA = 0.8
TAU = 0.5
KMAX = 2.0
BLK = 256
HIGH = lax.Precision.HIGHEST
MESH = pl.DeviceIdType.MESH
F32 = jnp.float32
BF16 = jnp.bfloat16
NN = (((1,), (0,)), ((), ()))
NTD = (((1,), (1,)), ((), ()))


def ddot(a, b, dims=NN):
    return lax.dot_general(a, b, dims, precision=HIGH, preferred_element_type=F32)


def bdot(a, b, dims=NN):
    return lax.dot_general(a, b, dims, preferred_element_type=F32)


def split(a):
    hi = a.astype(BF16)
    return hi, (a - hi.astype(F32)).astype(BF16)


def left3(a):
    hi, lo = split(a)
    return jnp.concatenate([hi, lo, hi], axis=1)


def right3(b):
    hi, lo = split(b)
    return jnp.concatenate([hi, hi, lo], axis=0)


def rows_of(n):
    return lax.broadcasted_iota(jnp.int32, (n, 1), 0).astype(F32)


def cols_of(n):
    return lax.broadcasted_iota(jnp.int32, (1, n), 1).astype(F32)


def divmod_of(v, n):
    q = jnp.floor((v + 0.5) * (1.0 / n))
    return q, v - n * q


def where01(cond):
    return jnp.where(cond, 1.0, 0.0).astype(F32)


def pick(m, r, c, transposed=False):
    on_r = where01(r == cols_of(N)).astype(BF16)
    on_c = where01(rows_of(N) == c).astype(BF16)
    total = None
    for part in split(m):
        left = bdot(on_r, part, NTD if transposed else NN).astype(BF16)
        out = bdot(left, on_c)
        total = out if total is None else total + out
    return total


def lookup(row, labels):
    total = None
    for k in range(N):
        term = row[:, k : k + 1] * where01(labels == k)
        total = term if total is None else total + term
    return total


def sincos(x):
    n = jnp.floor(x * (2.0 / math.pi) + 0.5)
    y = ((x - n * 1.5703125) - n * 4.83751296997e-4) - n * 7.54978995489e-8
    z = y * y
    s = y + y * z * (-1.6666654611e-1 + z * (8.3321608736e-3 - z * 1.9515295891e-4))
    c = 1.0 - 0.5 * z + z * z * (4.166664568298827e-2 - z * (1.388731625493765e-3 - z * 2.443315711809948e-5))
    q = n - 4.0 * jnp.floor(n * 0.25)
    odd = (q == 1.0) | (q == 3.0)
    sin = jnp.where(odd, c, s) * jnp.where(q >= 2.0, -1.0, 1.0)
    cos = jnp.where(odd, s, c) * jnp.where((q == 1.0) | (q == 2.0), -1.0, 1.0)
    return sin, cos


def kernel(
    sizes, f_hbm, u_hbm, lam_hbm, bases_hbm, vals_hbm, obs_hbm, pts_hbm, hist_hbm,
    out_hbm, spec_ref,
    f_in, u_in, lam_ref, bases_ref, vals_ref, obs_ref, pts_ref, hist_ref,
    out_buf, u_s, f_s, r_s, trace_s, zsend_s, halo_r, z_r,
    pan_s, pan_r, new_s, new_r, er_s, ei_s, part_s, part_r,
    local_sem, hs_sem, hr_sem, ps_sem, pr_sem, ns_sem, nr_sem, ss_sem, sr_sem,
):
    n_flow, n_col, n_row, comps, nx, ny, nz, pan, n_obs, nh = sizes
    ey, ez = ny // N, nz // N
    own_obs = n_obs // n_row
    flow, col, row = (lax.axis_index(a) for a in ("flow", "col", "row"))
    n_fc = n_flow * n_col
    fc = flow * n_col + col

    def fc_peer(d):
        t = lax.rem(fc + d, n_fc)
        return (lax.div(t, n_col), lax.rem(t, n_col), row)

    def row_peer(d):
        return (flow, col, lax.rem(row + d, n_row))

    def each_fc(body):
        if n_fc <= 16:
            for d in range(1, n_fc):
                body(d)
        else:
            lax.fori_loop(1, n_fc, lambda d, c: (body(d), c)[1], 0)

    pairs = (
        (bases_hbm, bases_ref), (u_hbm, u_in), (pts_hbm, pts_ref), (hist_hbm, hist_ref),
        (f_hbm, f_in), (lam_hbm, lam_ref), (vals_hbm, vals_ref), (obs_hbm, obs_ref),
    )
    local = [pltpu.make_async_copy(a, b, local_sem.at[i]) for i, (a, b) in enumerate(pairs)]
    for copy in local:
        copy.start()
    halo_r[...] = jnp.zeros(halo_r.shape, F32)
    z_r[...] = jnp.zeros(z_r.shape, F32)
    barrier = pltpu.get_barrier_semaphore()
    each_fc(lambda d: pl.semaphore_signal(barrier, inc=1, device_id=fc_peer(d), device_id_type=MESH))
    for d in range(1, n_row):
        pl.semaphore_signal(barrier, inc=1, device_id=row_peer(d), device_id_type=MESH)

    local[0].wait()
    sx, sy, sz = bases_ref[0], bases_ref[1], bases_ref[2]

    def ends(m, labels):
        return lookup(m[0:1], labels), lookup(m[N - 1 : N], labels)

    hr = rows_of(nh)
    hc = cols_of(nh)
    ir, yr = divmod_of(hr, ny)
    er, jr = divmod_of(yr, N)
    ic, yc = divmod_of(hc, ny)
    ec, jc = divmod_of(yc, N)
    x0r, x5r = ends(sx, ic)
    y0r, y5r = ends(sy, jc)
    x0c, x5c = ends(sx, ir)
    y0c, y5c = ends(sy, jr)

    nc, myc = divmod_of(cols_of(nx * 16), 16)
    mec, mjc = divmod_of(myc, N)
    nr, myr = divmod_of(rows_of(nx * 16), 16)
    mer, mjr = divmod_of(myr, N)
    a_fwd = pick(sx, ir, nc, True) * pick(sy, jr, mjc, True) * where01((er == mec) & (myc < ny))
    lane = cols_of(BLK)
    inside = lane < nz
    zqr, zkr = divmod_of(rows_of(BLK), N)
    zqc, zkc = divmod_of(lane, N)
    z_fwd = pick(sz, zkr, zkc) * where01((zqr == zqc) & inside)
    a_fwd = left3(a_fwd)
    z_fwd = right3(z_fwd)

    z0r, z5r = ends(sz, zkc)
    z0c, z5c = ends(sz, zkr)
    kz = where01((zqr == zqc + 1) & inside & (zqr < ez)) * z0c * z5r
    kz = kz + where01((zqr == zqc - 1) & inside) * z5c * z0r
    first_lane = (lane >= nz) & (lane < nz + comps)
    last_lane = (lane >= nz + 8) & (lane < nz + 8 + comps)
    kz = kz + where01((zqr == 0) & first_lane) * z0c + where01((zqr == ez - 1) & last_lane) * z5c
    kz = right3(kz)

    ky = where01(ir == ic) * (
        where01(ec == er + 1) * y5c * y0r + where01(ec == er - 1) * y0c * y5r
    )
    t16, t8 = rows_of(16), rows_of(8)
    mxy = jnp.concatenate(
        [
            ky,
            where01(t16 == yc) * x0r,
            where01(t16 == yc) * x5r,
            where01((t8 == ic) & (ec == 0)) * y0r,
            where01((t8 == ic) & (ec == ey - 1)) * y5r,
        ],
        axis=0,
    )
    mxy = left3(mxy)
    hl = cols_of(48)
    inj = where01(hl == yr) * x5c + where01(hl == yr + 16) * x0c
    inj = inj + where01((hl == ir + 32) & (er == ey - 1)) * y5c
    inj = inj + where01((hl == ir + 40) & (er == 0)) * y0c
    inj = left3(inj)
    zin5 = jnp.where(zqc == ez - 1, z5r, 0.0)[:, 128:256]
    zin0 = jnp.where(zqc == 0, z0r, 0.0)[:, 0:128]

    def pan_copy(d):
        return pltpu.make_async_remote_copy(
            src_ref=pan_s, dst_ref=pan_r.at[d], send_sem=ps_sem.at[d], recv_sem=pr_sem.at[d],
            device_id=row_peer(d), device_id_type=MESH)

    def new_copy(d):
        return pltpu.make_async_remote_copy(
            src_ref=new_s, dst_ref=new_r.at[d], send_sem=ns_sem.at[d], recv_sem=nr_sem.at[d],
            device_id=row_peer(d), device_id_type=MESH)

    def part_copy(d):
        return pltpu.make_async_remote_copy(
            src_ref=part_s, dst_ref=part_r.at[fc], send_sem=ss_sem.at[d], recv_sem=sr_sem.at[d],
            device_id=fc_peer(d), device_id_type=MESH)

    def part_wait(d):
        src = lax.rem(fc + (n_fc - d), n_fc)
        pltpu.make_async_remote_copy(
            src_ref=part_s, dst_ref=part_r.at[src], send_sem=ss_sem.at[d], recv_sem=sr_sem.at[d],
            device_id=fc_peer(d), device_id_type=MESH).wait_recv()

    def faces(s):
        def copy(k, src, dst, where):
            return pltpu.make_async_remote_copy(
                src_ref=src, dst_ref=dst, send_sem=hs_sem.at[s, k], recv_sem=hr_sem.at[s, k],
                device_id=where, device_id_type=MESH)

        def rows(buf, a, n):
            return buf.at[s, pl.ds(a, n), :]

        return (
            (flow > 0, flow < n_flow - 1, copy(0, rows(trace_s, 0, 16), rows(halo_r, 0, 16), (flow - 1, col, row))),
            (flow < n_flow - 1, flow > 0, copy(1, rows(trace_s, 16, 16), rows(halo_r, 16, 16), (flow + 1, col, row))),
            (col > 0, col < n_col - 1, copy(2, rows(trace_s, 32, 8), rows(halo_r, 32, 8), (flow, col - 1, row))),
            (col < n_col - 1, col > 0, copy(3, rows(trace_s, 40, 8), rows(halo_r, 40, 8), (flow, col + 1, row))),
            (row > 0, row < n_row - 1, copy(4, zsend_s.at[s], z_r.at[s, 0], (flow, col, row - 1))),
            (row < n_row - 1, row > 0, copy(5, zsend_s.at[s], z_r.at[s, 1], (flow, col, row + 1))),
        )

    def forward(ref):
        fill = jnp.zeros((16 - ny, nz), F32)
        x = jnp.concatenate(
            [p for c in range(comps) for i in range(nx) for p in (ref[c, i], fill)], axis=0)
        x = jnp.concatenate([x, jnp.zeros((x.shape[0], BLK - nz), F32)], axis=1)
        y = bdot(left3(x), z_fwd)
        n = nx * 16
        return [bdot(a_fwd, right3(y[c * n : (c + 1) * n])) for c in range(comps)]

    def couple(parts, s, before_sends=None):
        pieces = [split(p) for p in parts]
        acc = None
        inner = []
        for c, (hi, lo) in enumerate(pieces):
            t = bdot(mxy, jnp.concatenate([hi, hi, lo], axis=0))
            trace_s[s, :, c * BLK : (c + 1) * BLK] = t[nh : nh + 48]
            inner.append(t[:nh])
        w = bdot(
            jnp.concatenate(
                [jnp.concatenate([p[h] for p in pieces], axis=0) for h in (0, 1, 0)], axis=1),
            kz)
        lanes = cols_of(128)
        for c in range(comps):
            wc = w[c * nh : (c + 1) * nh]
            keep = (lanes == nz - 128 + c) | (lanes == nz - 120 + c)
            piece = jnp.where(keep, wc[:, 128:256], 0.0)
            acc = piece if acc is None else acc + piece
            inner[c] = inner[c] + wc
        zsend_s[s] = acc
        if before_sends is not None:
            before_sends()
        for sends, _, copy in faces(s):
            pl.when(sends)(copy.start)
        return inner

    def finish(s):
        for _, receives, copy in faces(s):
            pl.when(receives)(copy.wait_recv)

    def update(parts, inner, s):
        zn, zp = z_r[s, 0], z_r[s, 1]
        r = r_s[...]
        new = []
        for c in range(comps):
            add = bdot(inj, right3(halo_r[s, :, c * BLK : (c + 1) * BLK]))
            zlo = zp[:, nz - 120 + c : nz - 119 + c] * zin0
            zhi = zn[:, nz - 128 + c : nz - 127 + c] * zin5
            total = inner[c] + add + jnp.concatenate([zlo, zhi], axis=1)
            new.append((1.0 - OMEGA) * parts[c] + r * (f_s[c] + TAU * total))
        return new

    local[1].wait()
    state = forward(u_in)
    inner = couple(
        state, 0, lambda: pl.semaphore_wait(barrier, (n_fc - 1) + (n_row - 1)))
    for c in range(comps):
        u_s[c] = state[c]

    local[2].wait()
    local[3].wait()
    pan_s[...] = jnp.zeros(pan_s.shape, F32)
    for n in range(NT - 1):
        pan_s[n * 4 : (n + 1) * 4, 0:pan] = hist_ref[n]
    pan_s[64:67, 0:pan] = pts_ref[...]
    narrow = pan_s[...]
    placed = narrow
    for i in range(1, n_row):
        placed = jnp.where(row == i, pltpu.roll(narrow, i * pan, 1), placed)
    pan_s[...] = placed
    for d in range(1, n_row):
        pan_copy(d).start()

    local[4].wait()
    for c, part in enumerate(forward(f_in)):
        f_s[c] = part
    for i in (5, 6, 7):
        local[i].wait()
    on_q = where01(rows_of(ez) == zqc).astype(BF16)
    lam2 = sum(bdot(p, on_q) for p in split(lam_ref[0]))
    den = lookup(vals_ref[0:1], ir) + lookup(vals_ref[1:2], jr) + lookup(vals_ref[2:3], zkc)
    for e in range(ey):
        den = den + where01(er == e) * lam2[e : e + 1]
    r_s[...] = jnp.where(inside, OMEGA / jnp.where(inside, den, 1.0), 0.0)

    a_back = pick(sx, nr, ic) * pick(sy, mjr, jc) * where01((mer == ec) & (myr < ny))
    a_back = left3(a_back)
    z_back = right3(pick(sz, zkr, zkc, True) * where01((zqr == zqc) & inside))
    zs = cols_of(128) - (row * pan).astype(F32)
    sq, sk = divmod_of(zs, N)
    z_new = pick(sz, zkr, sk, True) * where01((zqr == sq) & (zs >= 0) & (zs < pan))
    z_new = right3(z_new)
    own = where01(cols_of(n_obs) == rows_of(own_obs) + (row * own_obs).astype(F32))
    mine = ddot(own, obs_ref[...], NTD)
    half, freq = divmod_of(rows_of(2 * NF), NF)
    time, chan = divmod_of(cols_of(4 * NT), 4)
    sin_t, cos_t = sincos((freq + 0.5) * (math.pi / NF) * time)
    table = jnp.where(half == 0, cos_t, -sin_t)
    last = table[:, 4 * NT - 1 : 4 * NT]
    wide = jnp.concatenate([table * where01(chan == c) for c in range(4)], axis=0)

    finish(0)
    state = update([u_s[c] for c in range(comps)], inner, 0)
    inner = couple(state, 1)
    for c in range(comps):
        u_s[c] = state[c]

    for d in range(1, n_row):
        pan_copy(d).wait_recv()
    panels = pan_s[...]
    for d in range(1, n_row):
        panels = panels + pan_r[d]
    dx, dy, dz = (mine[:, a : a + 1] - panels[64 + a : 65 + a, :] for a in range(3))
    r2 = dx * dx + dy * dy + dz * dz
    radius = jnp.sqrt(r2)
    inv = 1.0 / radius
    dx, dy, dz = dx * inv, dy * inv, dz * inv
    amp = inv * (1.0 / (4.0 * math.pi))
    step = KMAX / NF
    sin_r, ar = sincos(radius * (0.5 * step))
    ai = -sin_r
    sr, si = ar * ar - ai * ai, 2.0 * ar * ai
    ar, ai = ar * amp, ai * amp
    spectral = ddot(wide, panels[0:64])
    lane128 = lax.broadcasted_iota(jnp.int32, (1, 128), 1)
    total = jnp.zeros((own_obs, 128), F32)
    for f in range(NF):
        k = step * (f + 0.5)
        er_s[f], ei_s[f] = ar, ai
        re = [spectral[2 * NF * c + f : 2 * NF * c + f + 1] for c in range(4)]
        im = [spectral[2 * NF * c + NF + f : 2 * NF * c + NF + f + 1] for c in range(4)]
        d_re = dx * re[1] + dy * re[2] + dz * re[3]
        d_im = dx * im[1] + dy * im[2] + dz * im[3]
        t_re = d_re * inv - k * (im[0] + d_im)
        t_im = d_im * inv + k * (re[0] + d_re)
        s_re = jnp.sum(ar * t_re - ai * t_im, axis=1, keepdims=True)
        s_im = jnp.sum(ar * t_im + ai * t_re, axis=1, keepdims=True)
        total = jnp.where(lane128 == f, s_re, total)
        total = jnp.where(lane128 == NF + f, s_im, total)
        if f < NF - 1:
            ar, ai = ar * sr - ai * si, ar * si + ai * sr

    finish(1)
    state = update([u_s[c] for c in range(comps)], inner, 1)
    pieces = [split(p) for p in state]
    corners = jnp.zeros((8, BLK), F32)
    for c in range(4):
        hi, lo = pieces[c]
        top = bdot(a_back[0:16], jnp.concatenate([hi, hi, lo], axis=0))[0:1]
        corners = jnp.where(t8 == c, top, corners)
    new_s[...] = bdot(left3(corners), z_new)
    for d in range(1, n_row):
        new_copy(d).start()

    w = bdot(
        jnp.concatenate(
            [jnp.concatenate([p[h] for p in pieces], axis=0) for h in (0, 1, 0)], axis=1),
        z_back)
    for c in range(comps):
        nodes = bdot(a_back, right3(w[c * nh : (c + 1) * nh]))
        for i in range(nx):
            out_buf[c, i] = nodes[i * 16 : i * 16 + ny, :nz]
    out_copy = pltpu.make_async_copy(out_buf, out_hbm, local_sem.at[8])
    out_copy.start()

    for d in range(1, n_row):
        new_copy(d).wait_recv()
    newest = new_s[...]
    for d in range(1, n_row):
        newest = newest + new_r[d]
    along = dx * newest[1:2] + dy * newest[2:3] + dz * newest[3:4]
    a_val = newest[0:1] + along
    b_val = along * inv
    fresh = jnp.zeros((own_obs, 128), F32)
    for f in range(NF):
        k = step * (f + 0.5)
        ka = k * a_val
        gr, gi = er_s[f], ei_s[f]
        s_re = jnp.sum(gr * b_val - gi * ka, axis=1, keepdims=True)
        s_im = jnp.sum(gr * ka + gi * b_val, axis=1, keepdims=True)
        fresh = jnp.where(lane128 == f, s_re, fresh)
        fresh = jnp.where(lane128 == NF + f, s_im, fresh)
    turned = jnp.concatenate([fresh, total], axis=0).T
    fr, fi = turned[0:NF], turned[NF : 2 * NF]
    c15, s15 = last[0:NF], last[NF : 2 * NF]
    part_re = c15 * fr - s15 * fi + pltpu.roll(fr, own_obs, 1)
    part_im = c15 * fi + s15 * fr + pltpu.roll(fi, own_obs, 1)
    part = jnp.where(lane128 < own_obs, part_re, pltpu.roll(part_im, own_obs, 1))
    part_s[...] = part
    part_r[fc] = part
    each_fc(lambda d: part_copy(d).start())
    each_fc(part_wait)
    if n_fc <= 16:
        spectra = part_r[0]
        for d in range(1, n_fc):
            spectra = spectra + part_r[d]
    else:
        spectra = lax.fori_loop(1, n_fc, lambda d, acc: acc + part_r[d], part_r[0])
    spec_ref[0] = spectra[:, :own_obs]
    spec_ref[1] = spectra[:, own_obs : 2 * own_obs]

    for s in range(SWEEPS):
        for sends, _, copy in faces(s):
            pl.when(sends)(copy.wait_send)
    for d in range(1, n_row):
        pan_copy(d).wait_send()
        new_copy(d).wait_send()
    each_fc(lambda d: part_copy(d).wait_send())
    out_copy.wait()


def on_device(forcing, previous, shift, bases, values, observers, points, history):
    n_flow, n_col, n_row = (lax.axis_size(a) for a in ("flow", "col", "row"))
    comps, nx, ny, nz = forcing.shape
    n_fc = n_flow * n_col
    pan = points.shape[1]
    n_obs = observers.shape[1]
    own_obs = n_obs // n_row
    nh = -(-nx * ny // 16) * 16
    sizes = (n_flow, n_col, n_row, comps, nx, ny, nz, pan, n_obs, nh)
    history = jnp.transpose(history, (1, 0, 2))
    vmem = pl.BlockSpec(memory_space=pltpu.VMEM)
    hbm = pl.BlockSpec(memory_space=pl.ANY)
    dma = pltpu.SemaphoreType.DMA
    return pl.pallas_call(
        functools.partial(kernel, sizes),
        out_shape=(
            jax.ShapeDtypeStruct(forcing.shape, F32),
            jax.ShapeDtypeStruct((2, NF, own_obs), F32),
        ),
        in_specs=[hbm] * 8,
        out_specs=(hbm, vmem),
        scratch_shapes=[
            pltpu.VMEM((comps, nx, ny, nz), F32),
            pltpu.VMEM((comps, nx, ny, nz), F32),
            pltpu.VMEM(shift.shape, F32),
            pltpu.VMEM(bases.shape, F32),
            pltpu.VMEM(values.shape, F32),
            pltpu.VMEM(observers.shape, F32),
            pltpu.VMEM(points.shape, F32),
            pltpu.VMEM(history.shape, F32),
            pltpu.VMEM((comps, nx, ny, nz), F32),
            pltpu.VMEM((comps, nh, BLK), F32),
            pltpu.VMEM((comps, nh, BLK), F32),
            pltpu.VMEM((nh, BLK), F32),
            pltpu.VMEM((SWEEPS, 48, comps * BLK), F32),
            pltpu.VMEM((SWEEPS, nh, 128), F32),
            pltpu.VMEM((SWEEPS, 48, comps * BLK), F32),
            pltpu.VMEM((SWEEPS, 2, nh, 128), F32),
            pltpu.VMEM((72, 128), F32),
            pltpu.VMEM((n_row, 72, 128), F32),
            pltpu.VMEM((8, 128), F32),
            pltpu.VMEM((n_row, 8, 128), F32),
            pltpu.VMEM((NF, own_obs, 128), F32),
            pltpu.VMEM((NF, own_obs, 128), F32),
            pltpu.VMEM((NF, 128), F32),
            pltpu.VMEM((n_fc, NF, 128), F32),
            dma((9,)),
            dma((SWEEPS, 6)),
            dma((SWEEPS, 6)),
            dma((n_row,)),
            dma((n_row,)),
            dma((n_row,)),
            dma((n_row,)),
            dma((n_fc,)),
            dma((n_fc,)),
        ],
        compiler_params=pltpu.CompilerParams(
            collective_id=0, has_side_effects=True, vmem_limit_bytes=60 * 1024 * 1024
        ),
    )(forcing, previous, shift, bases, values, observers, points, history)


def solution(mesh):
    return jax.shard_map(
        on_device,
        mesh=mesh,
        in_specs=(
            P(None, "flow", "col", "row"),
            P(None, "flow", "col", "row"),
            P("flow", "col", "row"),
            P(),
            P(),
            P(),
            P(None, ("flow", "col", "row")),
            P(None, None, ("flow", "col", "row")),
        ),
        out_specs=(P(None, "flow", "col", "row"), P(None, None, "row")),
        check_vma=False,
    )
```

time: 29 us -> 27.3 us (0.941)
  local copies, waits for them, and re-layouts: 4.25 us -> 2.47 us
    unnamed x17 -> x4, local copies, waits for them, and re-layouts: 4.25 us -> 2.47 us
where the time goes in v2:
time: 27.3 us; the launch traced here: 27.1 us
  Pallas kernels  24 us (88%)
  local copies, waits for them, and re-layouts  2.47 us (9%)
  between operations  0.65 us (2%)
    pallas_call x1, Pallas kernels, on_device(): pl.pallas_call(functools.partial(kernel, sizes), out_shape=(jax.ShapeDtyp...  24 us
    unnamed x4, local copies, waits for them, and re-layouts  2.47 us

profile of v2, /device:TPU:0, one launch (start us, length us, event | category | flops | bytes accessed | tf_op | source)
XLA Modules:
  0.0 27.1 jit_solution(6943110167241558790)
XLA Ops:
  0.6 24.0 %shard_map.95 = (f32[5,6,12,192]{3,2,1,0:T(8,128)}, f32[2,16,64]{2,1,0:T(8,128)}) custom-call(f32[5,6,12,192]{3,2,1,0:T(8,128)} %f_hbm.1, f32[5,6,12,192]{3,2,1,0:T(8,128)} %u_hbm.1, f32[1,2,32]{2,1,0:T(2,128)} %lam_hbm.1, f32[3,6,6]{2,1,0:T(8,128)} %bases_hbm.1, f32[3,6]{1,0:T(4,128)} %vals_hbm.1, f32[3,256]{1,0:T(4,128)} %obs_hbm.1, f32[3,32]{1,0:T(4,128)} %pts_hbm.1, ...), custom_call_target="tpu_custom_call" | custom-call | tf_op jit(solution)/shard_map/pallas_call | solution.py:466
  24.7 0.0 copy-start
  24.7 1.9 %copy.12 = f32[5,6,12,192]{3,2,1,0:T(8,128)} copy(f32[5,6,12,192]{3,2,1,0:T(8,128)} %get-tuple-element.4) | data formatting | bytes 552960
  26.5 0.0 copy-done
  26.5 0.6 %copy.13 = f32[2,16,64]{2,1,0:T(8,128)} copy(f32[2,16,64]{2,1,0:T(8,128)S(1)} %copy-done) | data formatting | bytes 16384
Async XLA Ops:
  24.7 1.9 %copy-start = (f32[2,16,64]{2,1,0:T(8,128)S(1)}, f32[2,16,64]{2,1,0:T(8,128)}, u32[]{:S(2)}) copy-start(f32[2,16,64]{2,1,0:T(8,128)} %get-tuple-element.5) | copy-start | bytes 24580

commit v3 on v2

--- a/solution.py
+++ b/solution.py
@@ -100,8 +100,8 @@
     sizes, f_hbm, u_hbm, lam_hbm, bases_hbm, vals_hbm, obs_hbm, pts_hbm, hist_hbm,
     out_hbm, spec_ref,
     f_in, u_in, lam_ref, bases_ref, vals_ref, obs_ref, pts_ref, hist_ref,
-    out_buf, u_s, f_s, r_s, trace_s, zsend_s, halo_r, z_r,
-    pan_s, pan_r, new_s, new_r, er_s, ei_s, part_s, part_r,
+    out_buf, u_s, f_s, r_s, x_s, x_r, trace_s, zsend_s, halo_r, z_r,
+    flat_s, pan_s, pan_r, new_s, new_r, er_s, ei_s, part_s, part_r,
     local_sem, hs_sem, hr_sem, ps_sem, pr_sem, ns_sem, nr_sem, ss_sem, sr_sem,
 ):
     n_flow, n_col, n_row, comps, nx, ny, nz, pan, n_obs, nh = sizes
@@ -133,6 +133,7 @@
     for copy in local:
         copy.start()
     halo_r[...] = jnp.zeros(halo_r.shape, F32)
+    x_r[...] = jnp.zeros(x_r.shape, F32)
     z_r[...] = jnp.zeros(z_r.shape, F32)
     barrier = pltpu.get_barrier_semaphore()
     each_fc(lambda d: pl.semaphore_signal(barrier, inc=1, device_id=fc_peer(d), device_id_type=MESH))
@@ -203,8 +204,14 @@
 
     def pan_copy(d):
         return pltpu.make_async_remote_copy(
-            src_ref=pan_s, dst_ref=pan_r.at[d], send_sem=ps_sem.at[d], recv_sem=pr_sem.at[d],
+            src_ref=pan_s, dst_ref=pan_r.at[row], send_sem=ps_sem.at[d], recv_sem=pr_sem.at[d],
             device_id=row_peer(d), device_id_type=MESH)
+
+    def pan_wait(d):
+        src = lax.rem(row + (n_row - d), n_row)
+        pltpu.make_async_remote_copy(
+            src_ref=pan_s, dst_ref=pan_r.at[src], send_sem=ps_sem.at[d], recv_sem=pr_sem.at[d],
+            device_id=row_peer(d), device_id_type=MESH).wait_recv()
 
     def new_copy(d):
         return pltpu.make_async_remote_copy(
@@ -232,10 +239,10 @@
             return buf.at[s, pl.ds(a, n), :]
 
         return (
-            (flow > 0, flow < n_flow - 1, copy(0, rows(trace_s, 0, 16), rows(halo_r, 0, 16), (flow - 1, col, row))),
-            (flow < n_flow - 1, flow > 0, copy(1, rows(trace_s, 16, 16), rows(halo_r, 16, 16), (flow + 1, col, row))),
-            (col > 0, col < n_col - 1, copy(2, rows(trace_s, 32, 8), rows(halo_r, 32, 8), (flow, col - 1, row))),
-            (col < n_col - 1, col > 0, copy(3, rows(trace_s, 40, 8), rows(halo_r, 40, 8), (flow, col + 1, row))),
+            (flow > 0, flow < n_flow - 1, copy(0, x_s.at[s, 0], x_r.at[s, 0], (flow - 1, col, row))),
+            (flow < n_flow - 1, flow > 0, copy(1, x_s.at[s, 1], x_r.at[s, 1], (flow + 1, col, row))),
+            (col > 0, col < n_col - 1, copy(2, rows(trace_s, 0, 8), rows(halo_r, 0, 8), (flow, col - 1, row))),
+            (col < n_col - 1, col > 0, copy(3, rows(trace_s, 8, 8), rows(halo_r, 8, 8), (flow, col + 1, row))),
             (row > 0, row < n_row - 1, copy(4, zsend_s.at[s], z_r.at[s, 0], (flow, col, row - 1))),
             (row < n_row - 1, row > 0, copy(5, zsend_s.at[s], z_r.at[s, 1], (flow, col, row + 1))),
         )
@@ -249,14 +256,54 @@
         n = nx * 16
         return [bdot(a_fwd, right3(y[c * n : (c + 1) * n])) for c in range(comps)]
 
+    tiles = 2 * -(-(comps + (comps + 1) // 2) // 2)
+    half_tiles = tiles // 2
+
+    def pack_x(faces_of, s, side):
+        lows = [t[:, :128] for t in faces_of]
+        highs = [t[:, 128:] for t in faces_of]
+        both = lows + [
+            highs[i] + pltpu.roll(highs[i + 1], 64, 1) if i + 1 < comps else highs[i]
+            for i in range(0, comps, 2)
+        ]
+        both = both + [jnp.zeros((16, 128), F32)] * (tiles - len(both))
+        for a in range(tiles):
+            x_s[s, side, :, a * 128 : (a + 1) * 128] = both[a][0:8]
+        for a in range(half_tiles):
+            b = tiles + a
+            x_s[s, side, :, b * 128 : (b + 1) * 128] = both[a][8:16] + pltpu.roll(
+                both[a + half_tiles][8:16], 4, 0)
+
+    def unpack_x(s, side):
+        def tile(a):
+            return x_r[s, side, :, a * 128 : (a + 1) * 128]
+
+        both = []
+        for a in range(tiles):
+            rest = tile(tiles + a % half_tiles)
+            if a >= half_tiles:
+                rest = pltpu.roll(rest, 4, 0)
+            both.append(jnp.concatenate([tile(a), rest], axis=0))
+        faces_of = []
+        for c in range(comps):
+            high = both[comps + c // 2]
+            if c % 2:
+                high = pltpu.roll(high, 64, 1)
+            faces_of.append(jnp.concatenate([both[c], high], axis=1))
+        return faces_of
+
     def couple(parts, s, before_sends=None):
         pieces = [split(p) for p in parts]
         acc = None
         inner = []
+        x_faces = []
         for c, (hi, lo) in enumerate(pieces):
             t = bdot(mxy, jnp.concatenate([hi, hi, lo], axis=0))
-            trace_s[s, :, c * BLK : (c + 1) * BLK] = t[nh : nh + 48]
+            trace_s[s, :, c * BLK : (c + 1) * BLK] = t[nh + 32 : nh + 48]
+            x_faces.append(t[nh : nh + 32])
             inner.append(t[:nh])
+        pack_x([t[:16] for t in x_faces], s, 0)
+        pack_x([t[16:] for t in x_faces], s, 1)
         w = bdot(
             jnp.concatenate(
                 [jnp.concatenate([p[h] for p in pieces], axis=0) for h in (0, 1, 0)], axis=1),
@@ -283,8 +330,10 @@
         zn, zp = z_r[s, 0], z_r[s, 1]
         r = r_s[...]
         new = []
+        below, above = unpack_x(s, 0), unpack_x(s, 1)
         for c in range(comps):
-            add = bdot(inj, right3(halo_r[s, :, c * BLK : (c + 1) * BLK]))
+            sides = [below[c], above[c], halo_r[s, :, c * BLK : (c + 1) * BLK]]
+            add = bdot(inj, right3(jnp.concatenate(sides, axis=0)))
             zlo = zp[:, nz - 120 + c : nz - 119 + c] * zin0
             zhi = zn[:, nz - 128 + c : nz - 127 + c] * zin5
             total = inner[c] + add + jnp.concatenate([zlo, zhi], axis=1)
@@ -300,15 +349,15 @@
 
     local[2].wait()
     local[3].wait()
-    pan_s[...] = jnp.zeros(pan_s.shape, F32)
+    flat_s[...] = jnp.zeros(flat_s.shape, F32)
     for n in range(NT - 1):
-        pan_s[n * 4 : (n + 1) * 4, 0:pan] = hist_ref[n]
-    pan_s[64:67, 0:pan] = pts_ref[...]
-    narrow = pan_s[...]
-    placed = narrow
-    for i in range(1, n_row):
-        placed = jnp.where(row == i, pltpu.roll(narrow, i * pan, 1), placed)
-    pan_s[...] = placed
+        flat_s[n * 4 : (n + 1) * 4, 0:pan] = hist_ref[n]
+    flat_s[64:67, 0:pan] = pts_ref[...]
+    packed = flat_s[0:24]
+    for g in (1, 2):
+        packed = packed + pltpu.roll(flat_s[g * 24 : (g + 1) * 24], g * pan, 1)
+    pan_s[...] = packed
+    pan_r[row] = packed
     for d in range(1, n_row):
         pan_copy(d).start()
 
@@ -347,10 +396,17 @@
         u_s[c] = state[c]
 
     for d in range(1, n_row):
-        pan_copy(d).wait_recv()
-    panels = pan_s[...]
-    for d in range(1, n_row):
-        panels = panels + pan_r[d]
+        pan_wait(d)
+    groups = []
+    for g in range(3):
+        group = jnp.zeros((24, 128), F32)
+        for i in range(n_row):
+            shift = ((i - g) * pan) % 128
+            moved = pan_r[i] if shift == 0 else pltpu.roll(pan_r[i], shift, 1)
+            here = (cols_of(128) >= i * pan) & (cols_of(128) < (i + 1) * pan)
+            group = jnp.where(here, moved, group)
+        groups.append(group)
+    panels = jnp.concatenate(groups, axis=0)
     dx, dy, dz = (mine[:, a : a + 1] - panels[64 + a : 65 + a, :] for a in range(3))
     r2 = dx * dx + dy * dy + dz * dz
     radius = jnp.sqrt(r2)
@@ -459,6 +515,7 @@
     own_obs = n_obs // n_row
     nh = -(-nx * ny // 16) * 16
     sizes = (n_flow, n_col, n_row, comps, nx, ny, nz, pan, n_obs, nh)
+    tiles = 2 * -(-(comps + (comps + 1) // 2) // 2)
     history = jnp.transpose(history, (1, 0, 2))
     vmem = pl.BlockSpec(memory_space=pltpu.VMEM)
     hbm = pl.BlockSpec(memory_space=pl.ANY)
@@ -469,7 +526,7 @@
             jax.ShapeDtypeStruct(forcing.shape, F32),
             jax.ShapeDtypeStruct((2, NF, own_obs), F32),
         ),
-        in_specs=[hbm] * 8,
+        in_specs=[pl.BlockSpec(memory_space=pltpu.HBM)] * 8,
         out_specs=(hbm, vmem),
         scratch_shapes=[
             pltpu.VMEM((comps, nx, ny, nz), F32),
@@ -484,12 +541,15 @@
             pltpu.VMEM((comps, nh, BLK), F32),
             pltpu.VMEM((comps, nh, BLK), F32),
             pltpu.VMEM((nh, BLK), F32),
-            pltpu.VMEM((SWEEPS, 48, comps * BLK), F32),
+            pltpu.VMEM((SWEEPS, 2, 8, tiles * 192), F32),
+            pltpu.VMEM((SWEEPS, 2, 8, tiles * 192), F32),
+            pltpu.VMEM((SWEEPS, 16, comps * BLK), F32),
             pltpu.VMEM((SWEEPS, nh, 128), F32),
-            pltpu.VMEM((SWEEPS, 48, comps * BLK), F32),
+            pltpu.VMEM((SWEEPS, 16, comps * BLK), F32),
             pltpu.VMEM((SWEEPS, 2, nh, 128), F32),
             pltpu.VMEM((72, 128), F32),
-            pltpu.VMEM((n_row, 72, 128), F32),
+            pltpu.VMEM((24, 128), F32),
+            pltpu.VMEM((n_row, 24, 128), F32),
             pltpu.VMEM((8, 128), F32),
             pltpu.VMEM((n_row, 8, 128), F32),
             pltpu.VMEM((NF, own_obs, 128), F32),

time: 27.3 us -> 26.7 us (0.978)
  Pallas kernels: 24 us -> 23.4 us
    pallas_call x1, Pallas kernels: 24 us -> 23.4 us  [on_device(): pl.pallas_call(functools.partial(kernel, sizes), out_shape=(jax.ShapeDtyp...]
where the time goes in v3:
time: 26.7 us; the launch traced here: 26.5 us
  Pallas kernels  23.4 us (88%)
  local copies, waits for them, and re-layouts  2.47 us (9%)
  between operations  0.65 us (2%)
    pallas_call x1, Pallas kernels, on_device(): pl.pallas_call(functools.partial(kernel, sizes), out_shape=(jax.ShapeDtyp...  23.4 us
    unnamed x4, local copies, waits for them, and re-layouts  2.47 us

profile of v3, /device:TPU:0, one launch (start us, length us, event | category | flops | bytes accessed | tf_op | source)
XLA Modules:
  0.0 26.5 jit_solution(5407266370768825203)
XLA Ops:
  0.6 23.4 %shard_map.95 = (f32[5,6,12,192]{3,2,1,0:T(8,128)}, f32[2,16,64]{2,1,0:T(8,128)}) custom-call(f32[5,6,12,192]{3,2,1,0:T(8,128)} %f_hbm.1, f32[5,6,12,192]{3,2,1,0:T(8,128)} %u_hbm.1, f32[1,2,32]{2,1,0:T(2,128)} %lam_hbm.1, f32[3,6,6]{2,1,0:T(8,128)} %bases_hbm.1, f32[3,6]{1,0:T(4,128)} %vals_hbm.1, f32[3,256]{1,0:T(4,128)} %obs_hbm.1, f32[3,32]{1,0:T(4,128)} %pts_hbm.1, ...), custom_call_target="tpu_custom_call" | custom-call | tf_op jit(solution)/shard_map/pallas_call | solution.py:523
  24.0 0.0 copy-start
  24.1 1.9 %copy.12 = f32[5,6,12,192]{3,2,1,0:T(8,128)} copy(f32[5,6,12,192]{3,2,1,0:T(8,128)} %get-tuple-element.4) | data formatting | bytes 552960
  25.9 0.0 copy-done
  25.9 0.6 %copy.13 = f32[2,16,64]{2,1,0:T(8,128)} copy(f32[2,16,64]{2,1,0:T(8,128)S(1)} %copy-done) | data formatting | bytes 16384
Async XLA Ops:
  24.0 1.9 %copy-start = (f32[2,16,64]{2,1,0:T(8,128)S(1)}, f32[2,16,64]{2,1,0:T(8,128)}, u32[]{:S(2)}) copy-start(f32[2,16,64]{2,1,0:T(8,128)} %get-tuple-element.5) | copy-start | bytes 24580

commit v4 on v3

--- a/solution.py
+++ b/solution.py
@@ -304,6 +304,10 @@
             inner.append(t[:nh])
         pack_x([t[:16] for t in x_faces], s, 0)
         pack_x([t[16:] for t in x_faces], s, 1)
+        if before_sends is not None:
+            before_sends()
+        for sends, _, copy in faces(s)[:4]:
+            pl.when(sends)(copy.start)
         w = bdot(
             jnp.concatenate(
                 [jnp.concatenate([p[h] for p in pieces], axis=0) for h in (0, 1, 0)], axis=1),
@@ -316,9 +320,7 @@
             acc = piece if acc is None else acc + piece
             inner[c] = inner[c] + wc
         zsend_s[s] = acc
-        if before_sends is not None:
-            before_sends()
-        for sends, _, copy in faces(s):
+        for sends, _, copy in faces(s)[4:]:
             pl.when(sends)(copy.start)
         return inner
 

time: 26.7 us -> 26.7 us (level)
  no operation moved by 1% of the time
where the time goes in v4:
time: 26.7 us; the launch traced here: 26.5 us
  Pallas kernels  23.4 us (88%)
  local copies, waits for them, and re-layouts  2.47 us (9%)
  between operations  0.65 us (2%)
    pallas_call x1, Pallas kernels, on_device(): pl.pallas_call(functools.partial(kernel, sizes), out_shape=(jax.ShapeDtyp...  23.4 us
    unnamed x4, local copies, waits for them, and re-layouts  2.47 us

profile of v4, /device:TPU:0, one launch (start us, length us, event | category | flops | bytes accessed | tf_op | source)
XLA Modules:
  0.0 26.5 jit_solution(11731873834372767402)
XLA Ops:
  0.6 23.4 %shard_map.95 = (f32[5,6,12,192]{3,2,1,0:T(8,128)}, f32[2,16,64]{2,1,0:T(8,128)}) custom-call(f32[5,6,12,192]{3,2,1,0:T(8,128)} %f_hbm.1, f32[5,6,12,192]{3,2,1,0:T(8,128)} %u_hbm.1, f32[1,2,32]{2,1,0:T(2,128)} %lam_hbm.1, f32[3,6,6]{2,1,0:T(8,128)} %bases_hbm.1, f32[3,6]{1,0:T(4,128)} %vals_hbm.1, f32[3,256]{1,0:T(4,128)} %obs_hbm.1, f32[3,32]{1,0:T(4,128)} %pts_hbm.1, ...), custom_call_target="tpu_custom_call" | custom-call | tf_op jit(solution)/shard_map/pallas_call | solution.py:525
  24.1 0.0 copy-start
  24.1 1.9 %copy.12 = f32[5,6,12,192]{3,2,1,0:T(8,128)} copy(f32[5,6,12,192]{3,2,1,0:T(8,128)} %get-tuple-element.4) | data formatting | bytes 552960
  25.9 0.0 copy-done
  25.9 0.6 %copy.13 = f32[2,16,64]{2,1,0:T(8,128)} copy(f32[2,16,64]{2,1,0:T(8,128)S(1)} %copy-done) | data formatting | bytes 16384
Async XLA Ops:
  24.1 1.9 %copy-start = (f32[2,16,64]{2,1,0:T(8,128)S(1)}, f32[2,16,64]{2,1,0:T(8,128)}, u32[]{:S(2)}) copy-start(f32[2,16,64]{2,1,0:T(8,128)} %get-tuple-element.5) | copy-start | bytes 24580
